TPU v7x, 512 devices: a whole 4x4x16 slice. The times are simulated.
512 devices in a mesh: dp: 32 (over x, z_lo, core), sample: 4 (over z_hi), mp: 4 (over y).
Axes of the slice: x: 4, y: 4, z: 16 (z_hi: 4, z_lo: 4; z = z_hi * 4 + z_lo), core: 2. Of those that a mesh axis runs over, the one named last changes fastest.
Arguments:
- prefix_hidden: bfloat16 [32, 832, 2048], P('dp', 'sample')
- prefix_kv_weight: bfloat16 [2048, 512], P(None, 'mp'), may hold values from -0.125 to 0.125
- action_hidden: bfloat16 [32, 1200, 1024], P('dp', 'sample'), may hold values from -6 to 6
- query_weight: bfloat16 [1024, 2048], P(None, 'mp'), may hold values from -0.1875 to 0.1875
- action_kv_weight: bfloat16 [1024, 512], replicated, may hold values from -0.1875 to 0.1875
- out_cotangent: bfloat16 [32, 1200, 2048], P('dp', 'sample', 'mp'), may hold values from -96 to 96
- prompt_len: int32 [32], P('dp'), may hold values from 1 to 64, as said below
- view_valid: int32 [32, 3], P('dp'), may hold values from 0 to 1, as said below
Outputs:
- prefix_grad: bfloat16 [32, 832, 2048], P('dp', ('sample', 'mp'))
- kv_weight_update: bfloat16 [2048, 512], P(None, 'mp')
Inputs may be any that keep to these rules, and one draw needn't show every extreme that they name: `prompt_len`: observation 0 uses all 64 prompt positions. `view_valid`: the first view of every observation is present.
All inputs are finite; a program needn't handle non-finite values.
Results may differ from a plain program's by a relative error of at most 0.012.
The roundings to bfloat16 on the way count: a program that leaves them out, or rounds other values in their place, can miss the bound.
Values may be sent and summed in bfloat16 or wider, within the bound.
A program may use at most 64 MiB of HBM per device.

v0:
```python
import jax
import jax.numpy as jnp
from jax import lax
from jax.sharding import PartitionSpec as P

HD = 256
VIEW_TOK = 256
HORIZON = 50


def prefix_valid(length, view_flags, total_rows):
    position = jnp.arange(total_rows, dtype=jnp.int32)
    image_end = view_flags.shape[0] * VIEW_TOK
    view_id = position // VIEW_TOK
    view_range = jnp.arange(view_flags.shape[0], dtype=jnp.int32)
    flag_of = jnp.sum(
        jnp.where(view_id[:, None] == view_range[None, :], view_flags[None, :], 0), axis=1
    )
    return jnp.where(position < image_end, flag_of == 1, position - image_end < length)


def attention_grads(queries, all_keys, all_values, grad_out, usable):
    row_total = queries.shape[0]
    prefix_rows = usable.shape[0]
    same_draw = jnp.arange(row_total, dtype=jnp.int32) // HORIZON
    allowed = jnp.concatenate(
        [
            jnp.broadcast_to(usable[None, :], (row_total, prefix_rows)),
            same_draw[:, None] == same_draw[None, :],
        ],
        axis=1,
    )
    scaling = HD ** (-0.5)
    scores = (
        jnp.einsum("qhd,kd->hqk", queries, all_keys, preferred_element_type=jnp.float32) * scaling
    )
    row_max = jnp.max(jnp.where(allowed[None], scores, -jnp.inf), axis=-1, keepdims=True)
    exponent = jnp.where(allowed[None], jnp.exp(scores - row_max), 0.0)
    softmax = exponent / jnp.sum(exponent, axis=-1, keepdims=True)
    d_probs = jnp.einsum("qhd,kd->hqk", grad_out, all_values, preferred_element_type=jnp.float32)
    row_dot = jnp.sum(softmax * d_probs, axis=-1, keepdims=True)
    d_scores = (softmax * (d_probs - row_dot) * scaling).astype(jnp.bfloat16)
    probs_low = softmax.astype(jnp.bfloat16)
    d_keys = jnp.einsum(
        "hqk,qhd->kd", d_scores[:, :, :prefix_rows], queries, preferred_element_type=jnp.float32
    )
    d_values = jnp.einsum(
        "hqk,qhd->kd", probs_low[:, :, :prefix_rows], grad_out, preferred_element_type=jnp.float32
    )
    return jnp.concatenate([d_keys, d_values], axis=1)


def per_device(
    prefix_hidden,
    prefix_kv_weight,
    action_hidden,
    query_weight,
    action_kv_weight,
    out_cotangent,
    prompt_len,
    view_valid,
):
    hidden = prefix_hidden[0]
    block_rows = hidden.shape[0]
    col_width = prefix_kv_weight.shape[1]
    groups = lax.axis_size("sample")
    columns = lax.axis_size("mp")
    kv_cols = jnp.dot(hidden, prefix_kv_weight, preferred_element_type=jnp.float32).astype(
        jnp.bfloat16
    )
    gathered = lax.all_gather(kv_cols[None], ("sample", "mp"), axis=0, tiled=True)
    blocks = gathered.reshape(groups, columns, block_rows, col_width).transpose(0, 2, 1, 3)
    blocks = blocks.reshape(groups * block_rows, columns * col_width)
    total_rows = groups * block_rows
    actions = action_hidden[0]
    action_rows = actions.shape[0]
    queries = jnp.dot(actions, query_weight, preferred_element_type=jnp.float32).astype(
        jnp.bfloat16
    )
    queries = queries.reshape(action_rows, -1, HD)
    action_kv = jnp.dot(actions, action_kv_weight, preferred_element_type=jnp.float32).astype(
        jnp.bfloat16
    )
    all_keys = jnp.concatenate([blocks[:, :HD], action_kv[:, :HD]], axis=0)
    all_values = jnp.concatenate([blocks[:, HD:], action_kv[:, HD:]], axis=0)
    usable = prefix_valid(prompt_len[0], view_valid[0], total_rows)
    grad_out = out_cotangent[0].reshape(action_rows, -1, HD)
    d_prefix = attention_grads(queries, all_keys, all_values, grad_out, usable)
    pieces = d_prefix.reshape(groups, block_rows, columns, col_width).transpose(0, 2, 1, 3)
    pieces = pieces.reshape(groups * columns, block_rows, col_width)
    own_grad = lax.psum_scatter(pieces, ("sample", "mp"), scatter_dimension=0, tiled=True)[
        0
    ].astype(jnp.bfloat16)
    input_grad = lax.psum_scatter(
        jnp.einsum("rc,dc->rd", own_grad, prefix_kv_weight, preferred_element_type=jnp.float32),
        "mp",
        scatter_dimension=0,
        tiled=True,
    )
    weight_term = jnp.einsum("rd,rc->dc", hidden, own_grad, preferred_element_type=jnp.float32)
    entries = weight_term.shape[0] * weight_term.shape[1] * columns
    weight_grad = lax.psum(weight_term, ("dp", "sample"))
    squares = lax.psum(jnp.sum(weight_grad * weight_grad), "mp")
    scaling = lax.rsqrt(squares / entries + 1e-06)
    update = (weight_grad * scaling).astype(jnp.bfloat16)
    return (input_grad.astype(jnp.bfloat16)[None], update)


def solution(mesh):
    return jax.shard_map(
        per_device,
        mesh=mesh,
        in_specs=(
            P("dp", "sample", None),
            P(None, "mp"),
            P("dp", "sample", None),
            P(None, "mp"),
            P(),
            P("dp", "sample", "mp"),
            P("dp"),
            P("dp", None),
        ),
        out_specs=(P("dp", ("sample", "mp"), None), P(None, "mp")),
        check_vma=False,
    )
```

profile of v0, /device:TPU:1, one launch (start us, length us, event | category | flops | bytes accessed | tf_op | source)
XLA Modules:
  0.0 561.0 jit_solution(2867805014228753544)
XLA Ops:
  7.2 0.0 copy-start
  7.2 0.0 reduce-scatter.4.cloned.1.call-start
  7.3 1.7 convolution_convert_fusion.2
  9.0 0.0 copy-start.8
  9.0 61.9 %all-gather = bf16[3328,128]{1,0:T(8,128)(2,1)S(1)} all-gather(bf16[208,128]{1,0:T(8,128)(2,1)S(1)} %convolution_convert_fusion.2), channel_id=2, replica_groups=mesh['dp'=32,'sample'=4,'mp'=4] {'sample','mp'}, dimensions={0}, use_global_device_ids=true | all-gather | bytes 905216 | tf_op jit(solution)/shard_map/all_gather | solution.py:71
  70.9 0.3 copy.30
  71.2 0.0 copy-start.7
  71.2 0.1 copy.49
  71.4 0.1 fusion.48
  71.4 0.0 copy-start.4
  71.5 0.0 copy-start.6
  71.5 0.5 convolution_convert_fusion.1
  72.0 0.7 fusion.49
  72.7 0.5 convolution_convert_fusion
  73.2 0.1 reshape.77
  73.3 0.1 broadcast_compare_fusion
  74.0 0.1 reshape_squeeze.3
  74.1 0.0 copy-done.6
  74.1 0.1 select_reduce_fusion.1
  74.3 0.2 pad_add_fusion
  74.5 0.6 fusion.10
  75.1 0.0 copy-start.5
  75.1 1.3 fusion.50
  76.4 0.0 copy-done.5
  76.4 0.9 multiply_reduce_fusion
  77.3 0.6 convolution_bitcast_fusion.2
  77.9 0.8 convolution_bitcast_fusion.3
  78.7 0.2 pad_maximum_fusion
  78.9 1.7 reshape.78
  80.6 2.8 copy.35
  83.5 0.0 reduce-scatter.4.cloned.1.call-update
  83.5 0.0 all-reduce.4.cloned.1.call-start
  83.5 122.9 %reduce-scatter.4.cloned.1.call-done = f32[1,208,128]{2,1,0:T(8,128)} async-done(((f32[16,208,128]{2,1,0:T(8,128)}), f32[1,208,128]{2,1,0:T(8,128)}) %reduce-scatter.4.cloned.1.call-update) | async-done | bytes 106512 | tf_op jit(solution)/shard_map/reduce_scatter | solution.py:91
  206.4 2.3 convolution_bitcast_fusion.1
  208.8 0.0 all-reduce.4.cloned.1.call-update
  208.8 0.0 copy-done.2
  208.8 0.4 fusion.33
  209.2 23.7 %fusion = f32[56,2048]{1,0:T(8,128)S(1)} fusion(f32[208,2048]{1,0:T(8,128)S(1)} %fusion.33), kind=kCustom, calls=%all-reduce-scatter | all-reduce-scatter fusion | flops 458753 | bytes 2164736
  232.9 2.0 collective-permute-start
  234.9 1.3 dynamic-slice.4
  236.9 0.0 collective-permute-done
  236.9 0.4 concatenate.16
  237.2 302.0 %all-reduce.4.cloned.1.call-done = f32[2048,128]{0,1:T(8,128)} async-done(((f32[2048,128]{0,1:T(8,128)}), f32[2048,128]{0,1:T(8,128)}) %all-reduce.4.cloned.1.call-update) | async-done | bytes 1048592 | tf_op jit(solution)/shard_map/psum | solution.py:102
  539.3 2.1 multiply_reduce_fusion.1
  541.4 0.7 fusion.31
  542.1 9.1 %psum.15 = f32[]{:T(128)} all-reduce(f32[]{:T(128)} %multiply_reduce_fusion.1), channel_id=1, replica_groups=mesh['dp'=32,'sample'=4,'mp'=4] {'mp'}, use_global_device_ids=true, to_apply=%region_8.9 | all-reduce | flops 1 | bytes 8 | tf_op jit(solution)/shard_map/psum | solution.py:103
  551.9 1.3 multiply_convert_fusion
  553.2 1.0 copy.36
  (14 shorter events, 0.1 us)
Async XLA Ops:
  7.2 64.3 %copy-start = (bf16[1024,512]{1,0:T(8,128)(2,1)S(1)}, bf16[1024,512]{1,0:T(8,128)(2,1)}, u32[]{:S(2)}) copy-start(bf16[1024,512]{1,0:T(8,128)(2,1)} %param.12) | copy-start | bytes 3145732
  7.2 199.2 %reduce-scatter.4.cloned.1.call-start = ((), (), s32[]{:S(2)}) async-start(), calls=%async_computation.1 | async-start | bytes 1810432 | tf_op jit(solution)/shard_map/reduce_scatter | solution.py:91
  9.0 62.4 %copy-start.8 = (bf16[1,300,1024]{2,1,0:T(8,128)(2,1)S(1)}, bf16[1,300,1024]{2,1,0:T(8,128)(2,1)}, u32[]{:S(2)}) copy-start(bf16[1,300,1024]{2,1,0:T(8,128)(2,1)} %param.10) | copy-start | bytes 1843204
  71.2 1.5 copy-start.7
  71.4 2.6 copy-start.4
  71.5 2.7 copy-start.6
  75.1 1.3 copy-start.5
  80.6 125.8 %copy-start.1 = (bf16[1,208,2048]{2,1,0:T(8,128)(2,1)S(1)}, bf16[1,208,2048]{2,1,0:T(8,128)(2,1)}, u32[]{:S(2)}) copy-start(bf16[1,208,2048]{2,1,0:T(8,128)(2,1)} %param.8) | copy-start | bytes 2555908
  83.5 125.3 %copy-start.2 = (bf16[2048,128]{1,0:T(8,128)(2,1)S(1)}, bf16[2048,128]{1,0:T(8,128)(2,1)}, u32[]{:S(2)}) copy-start(bf16[2048,128]{1,0:T(8,128)(2,1)} %param.9) | copy-start | bytes 1572868
  83.5 455.8 %all-reduce.4.cloned.1.call-start = ((), (), s32[]{:S(2)}) async-start(), calls=%async_computation.2 | async-start | bytes 2097152 | tf_op jit(solution)/shard_map/psum | solution.py:102
  206.4 2.4 copy-start.3
  232.9 3.9 collective-permute-start
Sparse Core Ops, SparseCore 0:
  83.6 122.7 reduce-scatter.3
  209.9 329.3 all-reduce.3
where the time goes:
time: 563 us; the launch traced here: 561 us
  waiting for transfers between devices  425 us (75%)
  blocking collectives  94.6 us (17%)
  between operations  16.3 us (3%)
  local copies, waits for them, and re-layouts  9.4 us (2%)
  matrix products  8.29 us (1%)
    psum x1, waiting for transfers between devices, per_device(): weight_grad = lax.psum(weight_term, ('dp', 'sample'))  302 us
    reduce_scatter x1, waiting for transfers between devices, per_device(): lax.psum_scatter(pieces, ('sample', 'mp'), scatter_dimension=0, tiled=True)  123 us
    all_gather x1, blocking collectives, per_device(): lax.all_gather(kv_cols[None], ('sample', 'mp'), axis=0, tiled=True)  61.9 us
    unnamed x1, blocking collectives  23.7 us
  transfers between devices with their start and end apart: 3, of which 2 were waited for; matrix products, arithmetic and copies ran while one was open for 5% of the time, Pallas kernels for 0%

commit v1 on v0

v1 whole, which is shorter than its diff:
```python
import jax
import jax.numpy as jnp
from jax import lax
from jax.experimental import pallas as pl
from jax.experimental.pallas import tpu as pltpu
from jax.sharding import PartitionSpec as P

BF = jnp.bfloat16
F32 = jnp.float32
D = 2048
HD = 256
ROWS = 208
COLS = 128
ACT = 300
ACTP = 304
QR = 2 * ACTP
VIEW_TOK = 256
VIEWS = 3
HORIZON = 50
NEG = -3.0e38
HALF = ((0, 112), (112, 96))
N_SEMS = 160


def dot(a, b):
    return jnp.dot(a, b, preferred_element_type=F32)


def dot_nt(a, b):
    return lax.dot_general(a, b, (((1,), (1,)), ((), ())), preferred_element_type=F32)


def kernel(
    len_ref, view_ref, hid_h, w_h, act_h, wq_h, wakv_h, cot_h,
    o_grad, o_upd, o_sq,
    hid_v, wg, act_v, wq_v, wakv_v, cot_v, kv, akv, qs, gs, e_s, d_s, ea_s, da_s,
    dkv, st, yb,
    rr, zst, za0, za1, zb0, zb1, zc0, zc1, zsc0, zsc1,
    dres, gbuf, hx, hxt, tf, ts, zr, upd,
    sq, ysq, xs, xsq, ds, dr,
    lsem, ssem, rsem,
):
    dp = lax.axis_index("dp")
    s = lax.axis_index("sample")
    m = lax.axis_index("mp")
    x = dp // 8
    zl = lax.rem(dp, 8) // 2
    c = lax.rem(dp, 2)

    def at(a, k):
        return lax.rem(a + k, 4)

    z = s * 4 + zl

    def dev(kx=0, kz=0, ks=0, km=0, kc=0):
        cc = 1 - c if kc else c
        d = at(x, kx) * 8 + at(zl, kz) * 2 + cc
        return {"dp": d, "sample": at(s, ks), "mp": at(m, km)}

    along_z = [(ks, kz) for ks in (2, 1, 3, 0) for kz in (1, 2, 3, 0) if ks or kz]
    yp, ym = dev(km=1), dev(km=3)
    zp, zm = dev(ks=1), dev(ks=3)
    xp, xm = dev(kx=1), dev(kx=3)
    other = dev(kc=1)

    index = {}
    sent = []

    def number(name):
        return index.setdefault(name, len(index))

    def send(name, src, dst, device):
        i = number(name)
        copy = pltpu.make_async_remote_copy(
            src_ref=src, dst_ref=dst, send_sem=ssem.at[i], recv_sem=rsem.at[i],
            device_id=device, device_id_type=pl.DeviceIdType.MESH,
        )
        copy.start()
        sent.append(copy)

    def recv(name, dst, device=None):
        i = number(name)
        pltpu.make_async_remote_copy(
            src_ref=dst, dst_ref=dst, send_sem=ssem.at[i], recv_sem=rsem.at[i],
            device_id=other if device is None else device,
            device_id_type=pl.DeviceIdType.MESH,
        ).wait_recv()

    def drain(n):
        for copy in sent[:n]:
            copy.wait_send()
        del sent[:n]

    def col(k):
        return pl.ds(pl.multiple_of(at(m, k) * COLS, COLS), COLS)

    loads = [
        pltpu.make_async_copy(hid_h.at[0, 0:112], hid_v.at[0:112], lsem.at[0]),
        pltpu.make_async_copy(w_h, wg.at[:, col(0)], lsem.at[1]),
        pltpu.make_async_copy(act_h.at[0], act_v, lsem.at[2]),
        pltpu.make_async_copy(wq_h, wq_v, lsem.at[3]),
        pltpu.make_async_copy(wakv_h, wakv_v, lsem.at[4]),
        pltpu.make_async_copy(cot_h.at[0], cot_v, lsem.at[5]),
        pltpu.make_async_copy(hid_h.at[0, 112:208], hid_v.at[112:208], lsem.at[6]),
    ]
    for i in (1, 0, 6):
        loads[i].start()

    barrier = pltpu.get_barrier_semaphore()
    peers = [dev(km=k) for k in (1, 2, 3)] + [dev(ks=ks, kz=kz) for ks, kz in along_z] + [other]
    peers += [dev(kx=k, kc=kc) for k in (1, 2, 3) for kc in (0, 1)]
    for peer in peers:
        pl.semaphore_signal(
            barrier, inc=1, device_id=peer, device_id_type=pl.DeviceIdType.MESH
        )

    def kvh(r, h, k):
        r0, n = HALF[h]
        return kv.at[r, pl.ds(r0, n), col(k)]

    def ysend(r):
        block = kv.at[r, :, col(0)]
        for k in (2, 1, 3):
            send(f"y{r}{k}", block, block, dev(km=k))

    def ywait(r):
        for k in (1, 3, 2):
            recv(f"y{r}{k}", kv.at[r, :, col(4 - k)])

    loads[1].wait()
    loads[0].wait()
    for i in (2, 3, 5, 4):
        loads[i].start()
    kv[0, 0:112, col(0)] = dot(hid_v[0:112], wg[:, col(0)]).astype(BF)
    pl.semaphore_wait(barrier, len(peers))
    send("zp0", kvh(0, 0, 0), kvh(3, 0, 0), zp)
    loads[6].wait()
    kv[0, 112:208, col(0)] = dot(hid_v[112:208], wg[:, col(0)]).astype(BF)
    send("zm1", kvh(0, 1, 0), kvh(1, 1, 0), zm)
    send("zp1", kvh(0, 1, 0), kvh(3, 1, 0), zp)
    send("zm0", kvh(0, 0, 0), kvh(1, 0, 0), zm)
    ysend(0)

    def slot(rx, rc):
        return pl.ds((rx * 2 + rc) * ROWS, ROWS)

    def hidden_columns(kx, kc):
        j = at(x, kx) * 2 + (1 - c if kc else c)
        return pl.ds(pl.multiple_of(j * 256, 256), 256)

    def send_hidden(kx):
        for kc in (0, 1):
            send(f"hx{kx}{kc}", hid_v.at[:, hidden_columns(kx, kc)],
                 hx.at[slot(4 - kx, kc)], dev(kx=kx, kc=kc))

    send_hidden(1)
    send_hidden(3)
    send("hx01", hid_v.at[:, hidden_columns(0, 1)], hx.at[slot(0, 1)], other)
    hx[slot(0, 0), :] = hid_v[:, hidden_columns(0, 0)]

    for ref in (qs, gs):
        ref[288:304, :] = jnp.zeros((16, HD), BF)
        ref[592:608, :] = jnp.zeros((16, HD), BF)
    akv[288:304, :] = jnp.zeros((16, 2 * HD), BF)
    loads[2].wait()
    loads[3].wait()
    queries = (dot(act_v[...], wq_v[...]).astype(BF).astype(F32) * (HD**-0.5)).astype(BF)
    qs[0:ACT, :] = queries[:, :HD]
    qs[ACTP : ACTP + ACT, :] = queries[:, HD:]
    loads[4].wait()
    akv[0:ACT, :] = dot(act_v[...], wakv_v[...]).astype(BF)
    loads[5].wait()
    gs[0:ACT, :] = cot_v[:, :HD]
    gs[ACTP : ACTP + ACT, :] = cot_v[:, HD:]

    block_max, block_sum, block_dot = {}, {}, {}

    def attend(r, keys, values, mask, e_ref, d_ref):
        scores = mask(dot_nt(keys, qs[...]))
        top = jnp.max(scores, axis=0, keepdims=True)
        e = jnp.exp(scores - top)
        d = dot_nt(values, gs[...])
        if e_ref is not None:
            e_ref[...] = e
            d_ref[...] = d
        block_max[r] = top
        block_sum[r] = jnp.sum(e, axis=0, keepdims=True)
        block_dot[r] = jnp.sum(e * d, axis=0, keepdims=True)

    def draw(i):
        total = jnp.zeros_like(i)
        for t in range(1, ACTP // HORIZON + 1):
            total = total + jnp.where(i >= t * HORIZON, 1, 0)
        return total

    key_draw = draw(lax.broadcasted_iota(jnp.int32, (ACTP, 1), 0))
    query_index = lax.broadcasted_iota(jnp.int32, (1, QR), 1)
    query_draw = draw(query_index - jnp.where(query_index >= ACTP, ACTP, 0))
    attend(
        "a", akv[:, :HD], akv[:, HD:],
        lambda scores: jnp.where(key_draw == query_draw, scores, NEG), None, None,
    )

    def attend_prefix(r):
        p = at(s, r) * ROWS + lax.broadcasted_iota(jnp.int32, (ROWS, 1), 0)
        usable = jnp.where(p >= VIEWS * VIEW_TOK, jnp.where(p - VIEWS * VIEW_TOK < len_ref[0], 1, 0), 0)
        for v in range(VIEWS):
            inside = jnp.where(p >= v * VIEW_TOK, 1, 0) * jnp.where(p < (v + 1) * VIEW_TOK, 1, 0)
            usable = usable + inside * jnp.where(view_ref[0, v] == 1, 1, 0)
        ceiling = jnp.where(usable > 0, -NEG, NEG)
        attend(
            r, kv[r, :, :HD], kv[r, :, HD:],
            lambda scores: jnp.minimum(scores, ceiling), e_s.at[r], d_s.at[r],
        )

    recv("zp0", kvh(3, 0, 0))
    send("zfp", kvh(3, 0, 0), kvh(2, 0, 0), zp)
    recv("zm1", kvh(1, 1, 0))
    send("zfm", kvh(1, 1, 0), kvh(2, 1, 0), zm)
    recv("zp1", kvh(3, 1, 0))
    ysend(3)
    recv("zm0", kvh(1, 0, 0))
    ysend(1)
    ywait(0)
    attend_prefix(0)
    recv("zfp", kvh(2, 0, 0))
    recv("zfm", kvh(2, 1, 0))
    ysend(2)
    send_hidden(2)
    ywait(3)
    attend_prefix(3)
    ywait(1)
    attend_prefix(1)
    ywait(2)
    attend_prefix(2)

    blocks = ("a", 0, 1, 2, 3)
    top = block_max["a"]
    for r in (0, 1, 2, 3):
        top = jnp.maximum(top, block_max[r])
    factor = {r: jnp.exp(block_max[r] - top) for r in blocks}
    total = sum(factor[r] * block_sum[r] for r in blocks)
    inverse = 1.0 / total
    row_dot = sum(factor[r] * block_dot[r] for r in blocks) * inverse

    def half(h):
        r0, n = HALF[h]
        return pl.ds(r0, n)

    def gradients(r):
        p = e_s[r] * (factor[r] * inverse)
        d = p * (d_s[r] - row_dot)
        dk = dot(d.astype(BF), qs[...])
        dv = dot(p.astype(BF), gs[...])
        dkv[r, :, :HD] = dk
        dkv[r, :, HD:] = dv
        st[r, :, :HD] = dk.astype(BF)
        st[r, :, HD:] = dv.astype(BF)
        for k in (2, 1, 3):
            send(f"r{r}{k}", st.at[r, :, col(k)], yb.at[r, 3 - k], dev(km=k))

    def finish(r):
        piece = dkv[r, :, col(0)]
        for k in (1, 3, 2):
            recv(f"r{r}{k}", yb.at[r, 3 - k])
            piece = piece + yb[r, 3 - k].astype(F32)
        rr[r] = piece
        if r:
            zst[r] = piece.astype(BF)

    gradients(2)
    gradients(1)
    gradients(3)
    gradients(0)
    finish(2)
    send("zap", zst.at[2, half(0)], za0, zp)
    send("zam", zst.at[2, half(1)], za1, zm)
    finish(1)
    send("zbp", zst.at[1, half(1)], zb1, zp)
    finish(3)
    send("zbm", zst.at[3, half(0)], zb0, zm)
    early = len(sent)
    recv("zap", za0)
    zsc0[...] = (rr[1, half(0), :] + za0[...].astype(F32)).astype(BF)
    send("zcp", zsc0, zc0, zp)
    recv("zam", za1)
    zsc1[...] = (rr[3, half(1), :] + za1[...].astype(F32)).astype(BF)
    send("zcm", zsc1, zc1, zm)

    def wpart(q, k):
        return wg.at[pl.ds(pl.multiple_of(c * 1024 + q * 512, 512), 512), col(k)]

    send("wp0", wpart(0, 0), wpart(0, 0), yp)
    send("wm1", wpart(1, 0), wpart(1, 0), ym)
    send("wp1", wpart(1, 0), wpart(1, 0), yp)
    send("wm0", wpart(0, 0), wpart(0, 0), ym)

    finish(0)
    for kx in (1, 3, 2):
        for kc in (0, 1):
            recv(f"hx{kx}{kc}", hx.at[slot(4 - kx, kc)])
    recv("hx01", hx.at[slot(0, 1)])
    hxt[...] = hx[...].T
    drain(early)

    def gh(rx, rc, h):
        r0, n = HALF[h]
        return gbuf.at[pl.ds((rx * 2 + rc) * ROWS + r0, n)]

    recv("zbm", zb0)
    recv("zcp", zc0)
    dres[half(0), :] = rr[0, half(0), :] + zb0[...].astype(F32) + zc0[...].astype(F32)
    gbuf[half(0), :] = dres[half(0), :].astype(BF)
    for kx in (2, 1, 3):
        send(f"g{kx}0", gh(0, 0, 0), gh(4 - kx, 0, 0), dev(kx=kx))
    send("gc00", gh(0, 0, 0), gh(0, 1, 0), other)
    recv("zbp", zb1)
    recv("zcm", zc1)
    dres[half(1), :] = rr[0, half(1), :] + zb1[...].astype(F32) + zc1[...].astype(F32)
    gbuf[half(1), :] = dres[half(1), :].astype(BF)
    for kx in (2, 1, 3):
        send(f"g{kx}1", gh(0, 0, 1), gh(4 - kx, 0, 1), dev(kx=kx))
    send("gc01", gh(0, 0, 1), gh(0, 1, 1), other)

    for k in range(4):
        ds[k, 0:52, :] = dres[52 * k : 52 * k + 52, :].astype(BF)
        ds[k, 48:64, :] = jnp.where(
            lax.broadcasted_iota(jnp.int32, (16, COLS), 0) < 4, ds[k, 48:64, :].astype(F32), 0.0
        ).astype(BF)
    for k in (1, 3, 2):
        send(f"dy{k}", ds.at[at(m, k)], dr.at[:, col(0)], dev(km=k))
    dr[:, col(0)] = ds[m]

    for h in (0, 1):
        for kx in (1, 3, 2):
            recv(f"g{kx}{h}", gh(4 - kx, 0, h))
            send(f"gc{kx}{h}", gh(4 - kx, 0, h), gh(4 - kx, 1, h), other)
    recv("wp0", wpart(0, 3))
    send("wfp", wpart(0, 3), wpart(0, 3), yp)
    recv("wm1", wpart(1, 1))
    send("wfm", wpart(1, 1), wpart(1, 1), ym)
    recv("gc00", gh(0, 1, 0))
    recv("gc01", gh(0, 1, 1))
    for h in (0, 1):
        for kx in (1, 3, 2):
            recv(f"gc{kx}{h}", gh(4 - kx, 1, h))

    tf[...] = dot(hxt[...], gbuf[...])
    ts[...] = tf[...].astype(BF)

    def rows(start, n):
        return pl.ds(pl.multiple_of(start, n), n)

    def place(ks, kz):
        return (at(s, ks) * 4 + at(zl, kz)) * 16

    for i, (ks, kz) in enumerate(along_z):
        send(f"t{ks}{kz}", ts.at[rows(place(ks, kz), 16)], zr.at[i], dev(ks=ks, kz=kz))
    recv("wp1", wpart(1, 3))
    recv("wm0", wpart(0, 1))
    recv("wfp", wpart(0, 2))
    recv("wfm", wpart(1, 2))
    for k in (1, 2, 3):
        piece = wg.at[pl.ds(pl.multiple_of(c * 1024, 1024), 1024), col(k)]
        send(f"wc{k}", piece, piece, other)

    late = len(sent)
    base = (x * 2 + c) * 256
    piece = tf[rows(z * 16, 16), :]
    for i, (ks, kz) in reversed(list(enumerate(along_z))):
        recv(f"t{ks}{kz}", zr.at[i])
        piece = piece + zr[i].astype(F32)
    mine = upd.at[rows(base + z * 16, 16)]
    mine[...] = piece.astype(BF)
    for ks, kz in along_z:
        send(f"u{ks}{kz}", mine, mine, dev(ks=ks, kz=kz))
    drain(late)

    def u64(kx, ks):
        return upd.at[rows(at(x, kx) * 512 + c * 256 + at(s, ks) * 64, 64)]

    def u256(kx, kc):
        return upd.at[rows(at(x, kx) * 512 + (1 - c if kc else c) * 256, 256)]

    for ks in (0, 1, 3, 2):
        for kz in (1, 2, 3, 0):
            if ks or kz:
                source = rows(base + place(4 - ks, 4 - kz), 16)
                recv(f"u{ks}{kz}", upd.at[source])
        for kx in (2, 1, 3):
            send(f"ux{kx}{ks}", u64(0, 4 - ks), u64(0, 4 - ks), dev(kx=kx))
    send("uc0", u256(0, 0), u256(0, 0), other)
    own = upd[rows(base, 256), :].astype(F32)
    sq[...] = jnp.sum((own * own).reshape(32, 8, COLS), axis=0)
    for k in (1, 3, 2):
        send(f"sy{k}", sq, ysq.at[3 - k], dev(km=k))

    for k in (1, 2, 3):
        piece = wg.at[pl.ds(pl.multiple_of((1 - c) * 1024, 1024), 1024), col(k)]
        recv(f"wc{k}", piece)
    for k in (1, 3, 2):
        recv(f"dy{k}", dr.at[:, col(4 - k)])
    for j in range(4):
        part = dot_nt(dr[...], wg[512 * j : 512 * j + 512, :])
        o_grad[0, :, 512 * j : 512 * j + 512] = part[:52].astype(BF)

    for k in (1, 3, 2):
        recv(f"sy{k}", ysq.at[3 - k])
    xs[...] = sq[...] + ysq[0] + ysq[1] + ysq[2]
    across = [(kx, kc) for kx in (2, 1, 3, 0) for kc in (1, 0) if kx or kc]
    for i, (kx, kc) in enumerate(across):
        send(f"sx{kx}{kc}", xs, xsq.at[i], dev(kx=kx, kc=kc))
    for kx in (1, 3, 2):
        for ks in (0, 1, 3, 2):
            recv(f"ux{kx}{ks}", u64(4 - kx, 4 - ks))
        send(f"uc{kx}", u256(4 - kx, 0), u256(4 - kx, 0), other)
    everything = xs[...]
    for i, (kx, kc) in enumerate(across):
        recv(f"sx{kx}{kc}", xsq.at[i])
        everything = everything + xsq[i]
    o_sq[...] = everything
    recv("uc0", u256(0, 1))
    for kx in (1, 3, 2):
        recv(f"uc{kx}", u256(4 - kx, 1))
    o_upd[...] = upd[...]
    drain(len(sent))


def write_results(grad_ref, raw_ref, sq_ref, o_grad, o_upd):
    o_grad[...] = grad_ref[...]
    scale = lax.rsqrt(jnp.sum(sq_ref[...]) / (D * 2 * HD) + 1e-06)
    o_upd[...] = (raw_ref[...].astype(F32) * scale).astype(BF)


def per_device(
    prefix_hidden, prefix_kv_weight, action_hidden, query_weight, action_kv_weight,
    out_cotangent, prompt_len, view_valid,
):
    vm = pltpu.VMEM
    scratch = [
        vm((ROWS, D), BF), vm((D, 512), BF), vm((ACT, 1024), BF), vm((1024, 512), BF),
        vm((1024, 512), BF), vm((ACT, 512), BF), vm((4, ROWS, 512), BF), vm((ACTP, 512), BF),
        vm((QR, HD), BF), vm((QR, HD), BF), vm((4, ROWS, QR), F32), vm((4, ROWS, QR), F32),
        vm((8, 128), F32), vm((8, 128), F32),
        vm((4, ROWS, 512), F32), vm((4, ROWS, 512), BF),
        vm((4, 3, ROWS, COLS), BF),
        vm((4, ROWS, COLS), F32), vm((4, ROWS, COLS), BF),
        vm((112, COLS), BF), vm((96, COLS), BF), vm((112, COLS), BF), vm((96, COLS), BF),
        vm((112, COLS), BF), vm((96, COLS), BF), vm((112, COLS), BF), vm((96, COLS), BF),
        vm((ROWS, COLS), F32), vm((8 * ROWS, COLS), BF), vm((8 * ROWS, 256), BF),
        vm((256, 8 * ROWS), BF), vm((256, COLS), F32), vm((256, COLS), BF),
        vm((15, 16, COLS), BF), vm((D, COLS), BF),
        vm((8, 128), F32), vm((3, 8, 128), F32), vm((8, 128), F32), vm((7, 8, 128), F32),
        vm((4, 64, COLS), BF), vm((64, 512), BF),
        pltpu.SemaphoreType.DMA((7,)),
        pltpu.SemaphoreType.DMA((N_SEMS,)), pltpu.SemaphoreType.DMA((N_SEMS,)),
    ]
    smem = pl.BlockSpec(memory_space=pltpu.SMEM)
    hbm = pl.BlockSpec(memory_space=pltpu.HBM)
    grad, raw, squares = pl.pallas_call(
        kernel,
        out_shape=(
            jax.ShapeDtypeStruct((1, 52, D), BF),
            jax.ShapeDtypeStruct((D, COLS), BF),
            jax.ShapeDtypeStruct((8, 128), F32),
        ),
        in_specs=[smem, smem] + [hbm] * 6,
        out_specs=(pl.BlockSpec(memory_space=pltpu.VMEM),) * 3,
        scratch_shapes=scratch,
        compiler_params=pltpu.CompilerParams(
            collective_id=0, has_side_effects=True, vmem_limit_bytes=40 * 1024 * 1024
        ),
    )(
        prompt_len, view_valid, *[pltpu.with_memory_space_constraint(v, pltpu.HBM) for v in (prefix_hidden, prefix_kv_weight, action_hidden, query_weight, action_kv_weight, out_cotangent)])
    return pl.pallas_call(
        write_results,
        out_shape=(
            jax.ShapeDtypeStruct((1, 52, D), BF),
            jax.ShapeDtypeStruct((D, COLS), BF),
        ),
        in_specs=[pl.BlockSpec(memory_space=pltpu.VMEM)] * 3,
        out_specs=(pl.BlockSpec(memory_space=pltpu.VMEM),) * 2,
        compiler_params=pltpu.CompilerParams(vmem_limit_bytes=40 * 1024 * 1024),
    )(grad, raw, squares)


def solution(mesh):
    return jax.shard_map(
        per_device,
        mesh=mesh,
        in_specs=(
            P("dp", "sample", None),
            P(None, "mp"),
            P("dp", "sample", None),
            P(None, "mp"),
            P(),
            P("dp", "sample", "mp"),
            P("dp"),
            P("dp", None),
        ),
        out_specs=(P("dp", ("sample", "mp"), None), P(None, "mp")),
        check_vma=False,
    )
```

time: 563 us -> 83.3 us (0.15)
  waiting for transfers between devices: 425 us -> 0 us
  blocking collectives: 94.6 us -> 0 us
  Pallas kernels: 0 us -> 81.8 us
  between operations: 16.3 us -> 1.31 us
  local copies, waits for them, and re-layouts: 9.4 us -> 0.01 us
  matrix products: 8.29 us -> 0 us
    psum x1 -> x0, waiting for transfers between devices: 302 us -> none  [per_device(): weight_grad = lax.psum(weight_term, ('dp', 'sample'))]
    reduce_scatter x1 -> x0, waiting for transfers between devices: 123 us -> none  [per_device(): lax.psum_scatter(pieces, ('sample', 'mp'), scatter_dimension=0, tiled=True)]
    pallas_call x0 -> x2, Pallas kernels: none -> 81.8 us  [the longest x1 80.7 us: per_device(): pl.pallas_call(kernel, out_shape=(jax.ShapeDtypeStruct((1, 52, D), BF), j...]
    all_gather x1 -> x0, blocking collectives: 61.9 us -> none  [per_device(): lax.all_gather(kv_cols[None], ('sample', 'mp'), axis=0, tiled=True)]
    unnamed x1 -> x0, blocking collectives: 23.7 us -> none
    psum x1 -> x0, blocking collectives: 9.06 us -> none  [per_device(): squares = lax.psum(jnp.sum(weight_grad * weight_grad), 'mp')]
    dot_general x9 -> x0, matrix products: 8.29 us -> none  [the longest x1 2.33 us: per_device(): jnp.einsum('rd,rc->dc', hidden, own_grad, preferred_element_type=jnp.floa...]
  transfers between devices with their start and end apart: 3 -> 0, of which waited for: 2 -> 0; matrix products, arithmetic and copies ran while one was open for 5% -> 0% of each run, Pallas kernels for 0% -> 0%
where the time goes in v1:
time: 83.3 us; the launch traced here: 83.1 us
  Pallas kernels  81.8 us (98%)
  between operations  1.31 us (2%)
    pallas_call x1, Pallas kernels, per_device(): pl.pallas_call(kernel, out_shape=(jax.ShapeDtypeStruct((1, 52, D), BF), j...  80.7 us

profile of v1, /device:TPU:1, one launch (start us, length us, event | category | flops | bytes accessed | tf_op | source)
XLA Modules:
  0.0 83.1 jit_solution(15059014467702771825)
XLA Ops:
  0.6 0.0 copy-start
  1.3 0.0 copy-done
  1.3 80.7 %shard_map.95 = (bf16[1,52,2048]{2,1,0:T(8,128)(2,1)S(1)}, bf16[2048,128]{1,0:T(8,128)(2,1)S(1)}, f32[8,128]{1,0:T(8,128)S(1)}) custom-call(s32[1]{0:T(128)S(6)} %copy.10.len_ref, s32[1,3]{1,0:T(1,128)S(1)} %copy-done, bf16[1,208,2048]{2,1,0:T(8,128)(2,1)} %hid_h.1, bf16[2048,128]{1,0:T(8,128)(2,1)} %w_h.1, bf16[1,300,1024]{2,1,0:T(8,128)(2,1)} %act_h.1, ...), custom_call_target="tpu_custom_call" | custom-call | tf_op jit(solution)/shard_map/pallas_call | solution.py:460
  82.0 1.1 %shard_map.96 = (bf16[1,52,2048]{2,1,0:T(8,128)(2,1)}, bf16[2048,128]{1,0:T(8,128)(2,1)}) custom-call(bf16[1,52,2048]{2,1,0:T(8,128)(2,1)S(1)} %get-tuple-element.5.grad_ref, bf16[2048,128]{1,0:T(8,128)(2,1)S(1)} %get-tuple-element.6.raw_ref, f32[8,128]{1,0:T(8,128)S(1)} %get-tuple-element.7.sq_ref), custom_call_target="tpu_custom_call" | custom-call | tf_op jit(solution)/shard_map/pallas_call | solution.py:475
Async XLA Ops:
  0.6 0.7 copy-start

commit v2 on v1

--- a/solution.py
+++ b/solution.py
@@ -19,11 +19,16 @@
 HORIZON = 50
 NEG = -3.0e38
 HALF = ((0, 112), (112, 96))
+PART = ((0, 64), (64, 48), (112, 48), (160, 48))
 N_SEMS = 160
 
 
 def dot(a, b):
     return jnp.dot(a, b, preferred_element_type=F32)
+
+
+def wide(*pieces):
+    return jnp.concatenate(pieces, axis=1)
 
 
 def dot_nt(a, b):
@@ -33,7 +38,7 @@
 def kernel(
     len_ref, view_ref, hid_h, w_h, act_h, wq_h, wakv_h, cot_h,
     o_grad, o_upd, o_sq,
-    hid_v, wg, act_v, wq_v, wakv_v, cot_v, kv, akv, qs, gs, e_s, d_s, ea_s, da_s,
+    hid_v, wg, act_v, wq_v, wakv_v, cot_v, kv, akv, qs, gs, e_s, d_s,
     dkv, st, yb,
     rr, zst, za0, za1, zb0, zb1, zc0, zc1, zsc0, zsc1,
     dres, gbuf, hx, hxt, tf, ts, zr, upd,
@@ -91,12 +96,9 @@
             copy.wait_send()
         del sent[:n]
 
-    def col(k):
-        return pl.ds(pl.multiple_of(at(m, k) * COLS, COLS), COLS)
-
     loads = [
         pltpu.make_async_copy(hid_h.at[0, 0:112], hid_v.at[0:112], lsem.at[0]),
-        pltpu.make_async_copy(w_h, wg.at[:, col(0)], lsem.at[1]),
+        pltpu.make_async_copy(w_h, wg.at[m], lsem.at[1]),
         pltpu.make_async_copy(act_h.at[0], act_v, lsem.at[2]),
         pltpu.make_async_copy(wq_h, wq_v, lsem.at[3]),
         pltpu.make_async_copy(wakv_h, wakv_v, lsem.at[4]),
@@ -114,31 +116,34 @@
             barrier, inc=1, device_id=peer, device_id_type=pl.DeviceIdType.MESH
         )
 
-    def kvh(r, h, k):
-        r0, n = HALF[h]
-        return kv.at[r, pl.ds(r0, n), col(k)]
+    def kvp(r, i):
+        r0, n = PART[i]
+        return kv.at[r, m, pl.ds(r0, n)]
 
     def ysend(r):
-        block = kv.at[r, :, col(0)]
+        block = kv.at[r, m]
         for k in (2, 1, 3):
             send(f"y{r}{k}", block, block, dev(km=k))
 
     def ywait(r):
         for k in (1, 3, 2):
-            recv(f"y{r}{k}", kv.at[r, :, col(4 - k)])
+            recv(f"y{r}{k}", kv.at[r, at(m, 4 - k)])
 
     loads[1].wait()
     loads[0].wait()
     for i in (2, 3, 5, 4):
         loads[i].start()
-    kv[0, 0:112, col(0)] = dot(hid_v[0:112], wg[:, col(0)]).astype(BF)
+    kv[0, m, 0:112, :] = dot(hid_v[0:112], wg[m]).astype(BF)
     pl.semaphore_wait(barrier, len(peers))
-    send("zp0", kvh(0, 0, 0), kvh(3, 0, 0), zp)
+    for i in (0, 1):
+        send(f"zp{i}", kvp(0, i), kvp(3, i), zp)
     loads[6].wait()
-    kv[0, 112:208, col(0)] = dot(hid_v[112:208], wg[:, col(0)]).astype(BF)
-    send("zm1", kvh(0, 1, 0), kvh(1, 1, 0), zm)
-    send("zp1", kvh(0, 1, 0), kvh(3, 1, 0), zp)
-    send("zm0", kvh(0, 0, 0), kvh(1, 0, 0), zm)
+    kv[0, m, 112:208, :] = dot(hid_v[112:208], wg[m]).astype(BF)
+    for i in (2, 3):
+        send(f"zm{i}", kvp(0, i), kvp(1, i), zm)
+    for i, j in ((2, 0), (3, 1)):
+        send(f"zp{i}", kvp(0, i), kvp(3, i), zp)
+        send(f"zm{j}", kvp(0, j), kvp(1, j), zm)
     ysend(0)
 
     def slot(rx, rc):
@@ -209,22 +214,25 @@
             usable = usable + inside * jnp.where(view_ref[0, v] == 1, 1, 0)
         ceiling = jnp.where(usable > 0, -NEG, NEG)
         attend(
-            r, kv[r, :, :HD], kv[r, :, HD:],
+            r, wide(kv[r, 0], kv[r, 1]), wide(kv[r, 2], kv[r, 3]),
             lambda scores: jnp.minimum(scores, ceiling), e_s.at[r], d_s.at[r],
         )
 
-    recv("zp0", kvh(3, 0, 0))
-    send("zfp", kvh(3, 0, 0), kvh(2, 0, 0), zp)
-    recv("zm1", kvh(1, 1, 0))
-    send("zfm", kvh(1, 1, 0), kvh(2, 1, 0), zm)
-    recv("zp1", kvh(3, 1, 0))
+    for i, j in ((0, 2), (1, 3)):
+        recv(f"zp{i}", kvp(3, i))
+        send(f"zf{i}", kvp(3, i), kvp(2, i), zp)
+        recv(f"zm{j}", kvp(1, j))
+        send(f"zf{j}", kvp(1, j), kvp(2, j), zm)
+    for i in (2, 3):
+        recv(f"zp{i}", kvp(3, i))
     ysend(3)
-    recv("zm0", kvh(1, 0, 0))
+    for i in (0, 1):
+        recv(f"zm{i}", kvp(1, i))
     ysend(1)
     ywait(0)
     attend_prefix(0)
-    recv("zfp", kvh(2, 0, 0))
-    recv("zfm", kvh(2, 1, 0))
+    for i in (0, 2, 1, 3):
+        recv(f"zf{i}", kvp(2, i))
     ysend(2)
     send_hidden(2)
     ywait(3)
@@ -252,15 +260,15 @@
         d = p * (d_s[r] - row_dot)
         dk = dot(d.astype(BF), qs[...])
         dv = dot(p.astype(BF), gs[...])
-        dkv[r, :, :HD] = dk
-        dkv[r, :, HD:] = dv
-        st[r, :, :HD] = dk.astype(BF)
-        st[r, :, HD:] = dv.astype(BF)
+        for k in range(4):
+            half_block = (dk, dv)[k // 2][:, (k % 2) * COLS : (k % 2 + 1) * COLS]
+            dkv[r, k] = half_block
+            st[r, k] = half_block.astype(BF)
         for k in (2, 1, 3):
-            send(f"r{r}{k}", st.at[r, :, col(k)], yb.at[r, 3 - k], dev(km=k))
+            send(f"r{r}{k}", st.at[r, at(m, k)], yb.at[r, 3 - k], dev(km=k))
 
     def finish(r):
-        piece = dkv[r, :, col(0)]
+        piece = dkv[r, m]
         for k in (1, 3, 2):
             recv(f"r{r}{k}", yb.at[r, 3 - k])
             piece = piece + yb[r, 3 - k].astype(F32)
@@ -288,7 +296,7 @@
     send("zcm", zsc1, zc1, zm)
 
     def wpart(q, k):
-        return wg.at[pl.ds(pl.multiple_of(c * 1024 + q * 512, 512), 512), col(k)]
+        return wg.at[at(m, k), pl.ds(pl.multiple_of(c * 1024 + q * 512, 512), 512)]
 
     send("wp0", wpart(0, 0), wpart(0, 0), yp)
     send("wm1", wpart(1, 0), wpart(1, 0), ym)
@@ -328,8 +336,8 @@
             lax.broadcasted_iota(jnp.int32, (16, COLS), 0) < 4, ds[k, 48:64, :].astype(F32), 0.0
         ).astype(BF)
     for k in (1, 3, 2):
-        send(f"dy{k}", ds.at[at(m, k)], dr.at[:, col(0)], dev(km=k))
-    dr[:, col(0)] = ds[m]
+        send(f"dy{k}", ds.at[at(m, k)], dr.at[m], dev(km=k))
+    dr[m] = ds[m]
 
     for h in (0, 1):
         for kx in (1, 3, 2):
@@ -361,7 +369,7 @@
     recv("wfp", wpart(0, 2))
     recv("wfm", wpart(1, 2))
     for k in (1, 2, 3):
-        piece = wg.at[pl.ds(pl.multiple_of(c * 1024, 1024), 1024), col(k)]
+        piece = wg.at[at(m, k), pl.ds(pl.multiple_of(c * 1024, 1024), 1024)]
         send(f"wc{k}", piece, piece, other)
 
     late = len(sent)
@@ -396,12 +404,13 @@
         send(f"sy{k}", sq, ysq.at[3 - k], dev(km=k))
 
     for k in (1, 2, 3):
-        piece = wg.at[pl.ds(pl.multiple_of((1 - c) * 1024, 1024), 1024), col(k)]
+        piece = wg.at[at(m, k), pl.ds(pl.multiple_of((1 - c) * 1024, 1024), 1024)]
         recv(f"wc{k}", piece)
     for k in (1, 3, 2):
-        recv(f"dy{k}", dr.at[:, col(4 - k)])
+        recv(f"dy{k}", dr.at[at(m, 4 - k)])
     for j in range(4):
-        part = dot_nt(dr[...], wg[512 * j : 512 * j + 512, :])
+        weight = wide(*[wg[k, 512 * j : 512 * j + 512, :] for k in range(4)])
+        part = dot_nt(wide(dr[0], dr[1], dr[2], dr[3]), weight)
         o_grad[0, :, 512 * j : 512 * j + 512] = part[:52].astype(BF)
 
     for k in (1, 3, 2):
@@ -438,11 +447,10 @@
 ):
     vm = pltpu.VMEM
     scratch = [
-        vm((ROWS, D), BF), vm((D, 512), BF), vm((ACT, 1024), BF), vm((1024, 512), BF),
-        vm((1024, 512), BF), vm((ACT, 512), BF), vm((4, ROWS, 512), BF), vm((ACTP, 512), BF),
+        vm((ROWS, D), BF), vm((4, D, COLS), BF), vm((ACT, 1024), BF), vm((1024, 512), BF),
+        vm((1024, 512), BF), vm((ACT, 512), BF), vm((4, 4, ROWS, COLS), BF), vm((ACTP, 512), BF),
         vm((QR, HD), BF), vm((QR, HD), BF), vm((4, ROWS, QR), F32), vm((4, ROWS, QR), F32),
-        vm((8, 128), F32), vm((8, 128), F32),
-        vm((4, ROWS, 512), F32), vm((4, ROWS, 512), BF),
+        vm((4, 4, ROWS, COLS), F32), vm((4, 4, ROWS, COLS), BF),
         vm((4, 3, ROWS, COLS), BF),
         vm((4, ROWS, COLS), F32), vm((4, ROWS, COLS), BF),
         vm((112, COLS), BF), vm((96, COLS), BF), vm((112, COLS), BF), vm((96, COLS), BF),
@@ -451,7 +459,7 @@
         vm((256, 8 * ROWS), BF), vm((256, COLS), F32), vm((256, COLS), BF),
         vm((15, 16, COLS), BF), vm((D, COLS), BF),
         vm((8, 128), F32), vm((3, 8, 128), F32), vm((8, 128), F32), vm((7, 8, 128), F32),
-        vm((4, 64, COLS), BF), vm((64, 512), BF),
+        vm((4, 64, COLS), BF), vm((4, 64, COLS), BF),
         pltpu.SemaphoreType.DMA((7,)),
         pltpu.SemaphoreType.DMA((N_SEMS,)), pltpu.SemaphoreType.DMA((N_SEMS,)),
     ]

time: 83.3 us -> 82.9 us (level)
  no operation moved by 1% of the time
where the time goes in v2:
time: 82.9 us; the launch traced here: 82.7 us
  Pallas kernels  81.4 us (98%)
  between operations  1.31 us (2%)
    pallas_call x1, Pallas kernels, per_device(): pl.pallas_call(kernel, out_shape=(jax.ShapeDtypeStruct((1, 52, D), BF), j...  80.3 us

profile of v2, /device:TPU:1, one launch (start us, length us, event | category | flops | bytes accessed | tf_op | source)
XLA Modules:
  0.0 82.7 jit_solution(10020570881373948700)
XLA Ops:
  0.6 0.0 copy-start
  1.3 0.0 copy-done
  1.3 80.3 %shard_map.95 = (bf16[1,52,2048]{2,1,0:T(8,128)(2,1)S(1)}, bf16[2048,128]{1,0:T(8,128)(2,1)S(1)}, f32[8,128]{1,0:T(8,128)S(1)}) custom-call(s32[1]{0:T(128)S(6)} %copy.10.len_ref, s32[1,3]{1,0:T(1,128)S(1)} %copy-done, bf16[1,208,2048]{2,1,0:T(8,128)(2,1)} %hid_h.1, bf16[2048,128]{1,0:T(8,128)(2,1)} %w_h.1, bf16[1,300,1024]{2,1,0:T(8,128)(2,1)} %act_h.1, ...), custom_call_target="tpu_custom_call" | custom-call | tf_op jit(solution)/shard_map/pallas_call | solution.py:468
  81.6 1.1 %shard_map.96 = (bf16[1,52,2048]{2,1,0:T(8,128)(2,1)}, bf16[2048,128]{1,0:T(8,128)(2,1)}) custom-call(bf16[1,52,2048]{2,1,0:T(8,128)(2,1)S(1)} %get-tuple-element.5.grad_ref, bf16[2048,128]{1,0:T(8,128)(2,1)S(1)} %get-tuple-element.6.raw_ref, f32[8,128]{1,0:T(8,128)S(1)} %get-tuple-element.7.sq_ref), custom_call_target="tpu_custom_call" | custom-call | tf_op jit(solution)/shard_map/pallas_call | solution.py:483
Async XLA Ops:
  0.6 0.7 copy-start

commit v3 on v2

--- a/solution.py
+++ b/solution.py
@@ -38,7 +38,7 @@
 def kernel(
     len_ref, view_ref, hid_h, w_h, act_h, wq_h, wakv_h, cot_h,
     o_grad, o_upd, o_sq,
-    hid_v, wg, act_v, wq_v, wakv_v, cot_v, kv, akv, qs, gs, e_s, d_s,
+    hid_v, wg, act_v, wq_v, wakv_v, cot_v, kv, akv, qs, gs, qt, gt, e_s, d_s,
     dkv, st, yb,
     rr, zst, za0, za1, zb0, zb1, zc0, zc1, zsc0, zsc1,
     dres, gbuf, hx, hxt, tf, ts, zr, upd,
@@ -178,13 +178,16 @@
     gs[0:ACT, :] = cot_v[:, :HD]
     gs[ACTP : ACTP + ACT, :] = cot_v[:, HD:]
 
+    qt[...] = qs[...].T
+    gt[...] = gs[...].T
+
     block_max, block_sum, block_dot = {}, {}, {}
 
     def attend(r, keys, values, mask, e_ref, d_ref):
-        scores = mask(dot_nt(keys, qs[...]))
+        scores = mask(dot(keys, qt[...]))
         top = jnp.max(scores, axis=0, keepdims=True)
         e = jnp.exp(scores - top)
-        d = dot_nt(values, gs[...])
+        d = dot(values, gt[...])
         if e_ref is not None:
             e_ref[...] = e
             d_ref[...] = d
@@ -197,6 +200,12 @@
         for t in range(1, ACTP // HORIZON + 1):
             total = total + jnp.where(i >= t * HORIZON, 1, 0)
         return total
+
+    for i, j in ((0, 2), (1, 3)):
+        recv(f"zp{i}", kvp(3, i))
+        send(f"zf{i}", kvp(3, i), kvp(2, i), zp)
+        recv(f"zm{j}", kvp(1, j))
+        send(f"zf{j}", kvp(1, j), kvp(2, j), zm)
 
     key_draw = draw(lax.broadcasted_iota(jnp.int32, (ACTP, 1), 0))
     query_index = lax.broadcasted_iota(jnp.int32, (1, QR), 1)
@@ -218,11 +227,6 @@
             lambda scores: jnp.minimum(scores, ceiling), e_s.at[r], d_s.at[r],
         )
 
-    for i, j in ((0, 2), (1, 3)):
-        recv(f"zp{i}", kvp(3, i))
-        send(f"zf{i}", kvp(3, i), kvp(2, i), zp)
-        recv(f"zm{j}", kvp(1, j))
-        send(f"zf{j}", kvp(1, j), kvp(2, j), zm)
     for i in (2, 3):
         recv(f"zp{i}", kvp(3, i))
     ysend(3)
@@ -384,6 +388,16 @@
         send(f"u{ks}{kz}", mine, mine, dev(ks=ks, kz=kz))
     drain(late)
 
+    for k in (1, 2, 3):
+        piece = wg.at[at(m, k), pl.ds(pl.multiple_of((1 - c) * 1024, 1024), 1024)]
+        recv(f"wc{k}", piece)
+    for k in (1, 3, 2):
+        recv(f"dy{k}", dr.at[at(m, 4 - k)])
+    for j in range(4):
+        weight = wide(*[wg[k, 512 * j : 512 * j + 512, :] for k in range(4)])
+        part = dot_nt(wide(dr[0], dr[1], dr[2], dr[3]), weight)
+        o_grad[0, :, 512 * j : 512 * j + 512] = part[:52].astype(BF)
+
     def u64(kx, ks):
         return upd.at[rows(at(x, kx) * 512 + c * 256 + at(s, ks) * 64, 64)]
 
@@ -402,16 +416,6 @@
     sq[...] = jnp.sum((own * own).reshape(32, 8, COLS), axis=0)
     for k in (1, 3, 2):
         send(f"sy{k}", sq, ysq.at[3 - k], dev(km=k))
-
-    for k in (1, 2, 3):
-        piece = wg.at[at(m, k), pl.ds(pl.multiple_of((1 - c) * 1024, 1024), 1024)]
-        recv(f"wc{k}", piece)
-    for k in (1, 3, 2):
-        recv(f"dy{k}", dr.at[at(m, 4 - k)])
-    for j in range(4):
-        weight = wide(*[wg[k, 512 * j : 512 * j + 512, :] for k in range(4)])
-        part = dot_nt(wide(dr[0], dr[1], dr[2], dr[3]), weight)
-        o_grad[0, :, 512 * j : 512 * j + 512] = part[:52].astype(BF)
 
     for k in (1, 3, 2):
         recv(f"sy{k}", ysq.at[3 - k])
@@ -428,6 +432,7 @@
         recv(f"sx{kx}{kc}", xsq.at[i])
         everything = everything + xsq[i]
     o_sq[...] = everything
+    drain(len(sent) - 3)
     recv("uc0", u256(0, 1))
     for kx in (1, 3, 2):
         recv(f"uc{kx}", u256(4 - kx, 1))
@@ -449,7 +454,8 @@
     scratch = [
         vm((ROWS, D), BF), vm((4, D, COLS), BF), vm((ACT, 1024), BF), vm((1024, 512), BF),
         vm((1024, 512), BF), vm((ACT, 512), BF), vm((4, 4, ROWS, COLS), BF), vm((ACTP, 512), BF),
-        vm((QR, HD), BF), vm((QR, HD), BF), vm((4, ROWS, QR), F32), vm((4, ROWS, QR), F32),
+        vm((QR, HD), BF), vm((QR, HD), BF), vm((HD, QR), BF), vm((HD, QR), BF),
+        vm((4, ROWS, QR), F32), vm((4, ROWS, QR), F32),
         vm((4, 4, ROWS, COLS), F32), vm((4, 4, ROWS, COLS), BF),
         vm((4, 3, ROWS, COLS), BF),
         vm((4, ROWS, COLS), F32), vm((4, ROWS, COLS), BF),

time: 82.9 us -> 82.9 us (level)
  no operation moved by 1% of the time
where the time goes in v3:
time: 82.9 us; the launch traced here: 82.7 us
  Pallas kernels  81.4 us (98%)
  between operations  1.31 us (2%)
    pallas_call x1, Pallas kernels, per_device(): pl.pallas_call(kernel, out_shape=(jax.ShapeDtypeStruct((1, 52, D), BF), j...  80.3 us

profile of v3, /device:TPU:1, one launch (start us, length us, event | category | flops | bytes accessed | tf_op | source)
XLA Modules:
  0.0 82.7 jit_solution(4401912796035986150)
XLA Ops:
  0.6 0.0 copy-start
  1.3 0.0 copy-done
  1.3 80.3 %shard_map.95 = (bf16[1,52,2048]{2,1,0:T(8,128)(2,1)S(1)}, bf16[2048,128]{1,0:T(8,128)(2,1)S(1)}, f32[8,128]{1,0:T(8,128)S(1)}) custom-call(s32[1]{0:T(128)S(6)} %copy.10.len_ref, s32[1,3]{1,0:T(1,128)S(1)} %copy-done, bf16[1,208,2048]{2,1,0:T(8,128)(2,1)} %hid_h.1, bf16[2048,128]{1,0:T(8,128)(2,1)} %w_h.1, bf16[1,300,1024]{2,1,0:T(8,128)(2,1)} %act_h.1, ...), custom_call_target="tpu_custom_call" | custom-call | tf_op jit(solution)/shard_map/pallas_call | solution.py:474
  81.6 1.1 %shard_map.96 = (bf16[1,52,2048]{2,1,0:T(8,128)(2,1)}, bf16[2048,128]{1,0:T(8,128)(2,1)}) custom-call(bf16[1,52,2048]{2,1,0:T(8,128)(2,1)S(1)} %get-tuple-element.5.grad_ref, bf16[2048,128]{1,0:T(8,128)(2,1)S(1)} %get-tuple-element.6.raw_ref, f32[8,128]{1,0:T(8,128)S(1)} %get-tuple-element.7.sq_ref), custom_call_target="tpu_custom_call" | custom-call | tf_op jit(solution)/shard_map/pallas_call | solution.py:489
Async XLA Ops:
  0.6 0.7 copy-start

commit v4 on v3

--- a/solution.py
+++ b/solution.py
@@ -18,8 +18,6 @@
 VIEWS = 3
 HORIZON = 50
 NEG = -3.0e38
-HALF = ((0, 112), (112, 96))
-PART = ((0, 64), (64, 48), (112, 48), (160, 48))
 N_SEMS = 160
 
 
@@ -40,7 +38,7 @@
     o_grad, o_upd, o_sq,
     hid_v, wg, act_v, wq_v, wakv_v, cot_v, kv, akv, qs, gs, qt, gt, e_s, d_s,
     dkv, st, yb,
-    rr, zst, za0, za1, zb0, zb1, zc0, zc1, zsc0, zsc1,
+    rr, zst, zb,
     dres, gbuf, hx, hxt, tf, ts, zr, upd,
     sq, ysq, xs, xsq, ds, dr,
     lsem, ssem, rsem,
@@ -63,9 +61,6 @@
         return {"dp": d, "sample": at(s, ks), "mp": at(m, km)}
 
     along_z = [(ks, kz) for ks in (2, 1, 3, 0) for kz in (1, 2, 3, 0) if ks or kz]
-    yp, ym = dev(km=1), dev(km=3)
-    zp, zm = dev(ks=1), dev(ks=3)
-    xp, xm = dev(kx=1), dev(kx=3)
     other = dev(kc=1)
 
     index = {}
@@ -116,10 +111,6 @@
             barrier, inc=1, device_id=peer, device_id_type=pl.DeviceIdType.MESH
         )
 
-    def kvp(r, i):
-        r0, n = PART[i]
-        return kv.at[r, m, pl.ds(r0, n)]
-
     def ysend(r):
         block = kv.at[r, m]
         for k in (2, 1, 3):
@@ -133,17 +124,11 @@
     loads[0].wait()
     for i in (2, 3, 5, 4):
         loads[i].start()
-    kv[0, m, 0:112, :] = dot(hid_v[0:112], wg[m]).astype(BF)
+    loads[6].wait()
+    kv[0, m] = dot(hid_v[...], wg[m]).astype(BF)
     pl.semaphore_wait(barrier, len(peers))
-    for i in (0, 1):
-        send(f"zp{i}", kvp(0, i), kvp(3, i), zp)
-    loads[6].wait()
-    kv[0, m, 112:208, :] = dot(hid_v[112:208], wg[m]).astype(BF)
-    for i in (2, 3):
-        send(f"zm{i}", kvp(0, i), kvp(1, i), zm)
-    for i, j in ((2, 0), (3, 1)):
-        send(f"zp{i}", kvp(0, i), kvp(3, i), zp)
-        send(f"zm{j}", kvp(0, j), kvp(1, j), zm)
+    for k in (2, 1, 3):
+        send(f"z{k}", kv.at[0, m], kv.at[4 - k, m], dev(ks=k))
     ysend(0)
 
     def slot(rx, rc):
@@ -201,12 +186,6 @@
             total = total + jnp.where(i >= t * HORIZON, 1, 0)
         return total
 
-    for i, j in ((0, 2), (1, 3)):
-        recv(f"zp{i}", kvp(3, i))
-        send(f"zf{i}", kvp(3, i), kvp(2, i), zp)
-        recv(f"zm{j}", kvp(1, j))
-        send(f"zf{j}", kvp(1, j), kvp(2, j), zm)
-
     key_draw = draw(lax.broadcasted_iota(jnp.int32, (ACTP, 1), 0))
     query_index = lax.broadcasted_iota(jnp.int32, (1, QR), 1)
     query_draw = draw(query_index - jnp.where(query_index >= ACTP, ACTP, 0))
@@ -227,24 +206,15 @@
             lambda scores: jnp.minimum(scores, ceiling), e_s.at[r], d_s.at[r],
         )
 
-    for i in (2, 3):
-        recv(f"zp{i}", kvp(3, i))
-    ysend(3)
-    for i in (0, 1):
-        recv(f"zm{i}", kvp(1, i))
-    ysend(1)
+    for r in (1, 3, 2):
+        recv(f"z{4 - r}", kv.at[r, m])
+        ysend(r)
     ywait(0)
     attend_prefix(0)
-    for i in (0, 2, 1, 3):
-        recv(f"zf{i}", kvp(2, i))
-    ysend(2)
     send_hidden(2)
-    ywait(3)
-    attend_prefix(3)
-    ywait(1)
-    attend_prefix(1)
-    ywait(2)
-    attend_prefix(2)
+    for r in (1, 3, 2):
+        ywait(r)
+        attend_prefix(r)
 
     blocks = ("a", 0, 1, 2, 3)
     top = block_max["a"]
@@ -254,10 +224,6 @@
     total = sum(factor[r] * block_sum[r] for r in blocks)
     inverse = 1.0 / total
     row_dot = sum(factor[r] * block_dot[r] for r in blocks) * inverse
-
-    def half(h):
-        r0, n = HALF[h]
-        return pl.ds(r0, n)
 
     def gradients(r):
         p = e_s[r] * (factor[r] * inverse)
@@ -284,28 +250,16 @@
     gradients(1)
     gradients(3)
     gradients(0)
-    finish(2)
-    send("zap", zst.at[2, half(0)], za0, zp)
-    send("zam", zst.at[2, half(1)], za1, zm)
-    finish(1)
-    send("zbp", zst.at[1, half(1)], zb1, zp)
-    finish(3)
-    send("zbm", zst.at[3, half(0)], zb0, zm)
+    for r in (2, 1, 3):
+        finish(r)
+        send(f"zr{r}", zst.at[r], zb.at[3 - r], dev(ks=r))
     early = len(sent)
-    recv("zap", za0)
-    zsc0[...] = (rr[1, half(0), :] + za0[...].astype(F32)).astype(BF)
-    send("zcp", zsc0, zc0, zp)
-    recv("zam", za1)
-    zsc1[...] = (rr[3, half(1), :] + za1[...].astype(F32)).astype(BF)
-    send("zcm", zsc1, zc1, zm)
-
-    def wpart(q, k):
-        return wg.at[at(m, k), pl.ds(pl.multiple_of(c * 1024 + q * 512, 512), 512)]
-
-    send("wp0", wpart(0, 0), wpart(0, 0), yp)
-    send("wm1", wpart(1, 0), wpart(1, 0), ym)
-    send("wp1", wpart(1, 0), wpart(1, 0), yp)
-    send("wm0", wpart(0, 0), wpart(0, 0), ym)
+
+    def wpart(half, k):
+        return wg.at[at(m, k), pl.ds(pl.multiple_of(half * 1024, 1024), 1024)]
+
+    for k in (2, 1, 3):
+        send(f"w{k}", wpart(c, 0), wpart(c, 0), dev(km=k))
 
     finish(0)
     for kx in (1, 3, 2):
@@ -315,24 +269,18 @@
     hxt[...] = hx[...].T
     drain(early)
 
-    def gh(rx, rc, h):
-        r0, n = HALF[h]
-        return gbuf.at[pl.ds((rx * 2 + rc) * ROWS + r0, n)]
-
-    recv("zbm", zb0)
-    recv("zcp", zc0)
-    dres[half(0), :] = rr[0, half(0), :] + zb0[...].astype(F32) + zc0[...].astype(F32)
-    gbuf[half(0), :] = dres[half(0), :].astype(BF)
+    def block(rx, rc):
+        return gbuf.at[slot(rx, rc)]
+
+    total_block = rr[0]
+    for r in (1, 3, 2):
+        recv(f"zr{r}", zb.at[3 - r])
+        total_block = total_block + zb[3 - r].astype(F32)
+    dres[...] = total_block
+    gbuf[slot(0, 0), :] = total_block.astype(BF)
     for kx in (2, 1, 3):
-        send(f"g{kx}0", gh(0, 0, 0), gh(4 - kx, 0, 0), dev(kx=kx))
-    send("gc00", gh(0, 0, 0), gh(0, 1, 0), other)
-    recv("zbp", zb1)
-    recv("zcm", zc1)
-    dres[half(1), :] = rr[0, half(1), :] + zb1[...].astype(F32) + zc1[...].astype(F32)
-    gbuf[half(1), :] = dres[half(1), :].astype(BF)
-    for kx in (2, 1, 3):
-        send(f"g{kx}1", gh(0, 0, 1), gh(4 - kx, 0, 1), dev(kx=kx))
-    send("gc01", gh(0, 0, 1), gh(0, 1, 1), other)
+        send(f"g{kx}", block(0, 0), block(4 - kx, 0), dev(kx=kx))
+    send("gc0", block(0, 0), block(0, 1), other)
 
     for k in range(4):
         ds[k, 0:52, :] = dres[52 * k : 52 * k + 52, :].astype(BF)
@@ -343,19 +291,11 @@
         send(f"dy{k}", ds.at[at(m, k)], dr.at[m], dev(km=k))
     dr[m] = ds[m]
 
-    for h in (0, 1):
-        for kx in (1, 3, 2):
-            recv(f"g{kx}{h}", gh(4 - kx, 0, h))
-            send(f"gc{kx}{h}", gh(4 - kx, 0, h), gh(4 - kx, 1, h), other)
-    recv("wp0", wpart(0, 3))
-    send("wfp", wpart(0, 3), wpart(0, 3), yp)
-    recv("wm1", wpart(1, 1))
-    send("wfm", wpart(1, 1), wpart(1, 1), ym)
-    recv("gc00", gh(0, 1, 0))
-    recv("gc01", gh(0, 1, 1))
-    for h in (0, 1):
-        for kx in (1, 3, 2):
-            recv(f"gc{kx}{h}", gh(4 - kx, 1, h))
+    for kx in (1, 3, 2):
+        recv(f"g{kx}", block(4 - kx, 0))
+        send(f"gc{kx}", block(4 - kx, 0), block(4 - kx, 1), other)
+    for kx in (0, 1, 3, 2):
+        recv(f"gc{kx}", block((4 - kx) % 4, 1))
 
     tf[...] = dot(hxt[...], gbuf[...])
     ts[...] = tf[...].astype(BF)
@@ -368,14 +308,9 @@
 
     for i, (ks, kz) in enumerate(along_z):
         send(f"t{ks}{kz}", ts.at[rows(place(ks, kz), 16)], zr.at[i], dev(ks=ks, kz=kz))
-    recv("wp1", wpart(1, 3))
-    recv("wm0", wpart(0, 1))
-    recv("wfp", wpart(0, 2))
-    recv("wfm", wpart(1, 2))
-    for k in (1, 2, 3):
-        piece = wg.at[at(m, k), pl.ds(pl.multiple_of(c * 1024, 1024), 1024)]
-        send(f"wc{k}", piece, piece, other)
-
+    for k in (1, 3, 2):
+        recv(f"w{k}", wpart(c, 4 - k))
+        send(f"wc{k}", wpart(c, 4 - k), wpart(c, 4 - k), other)
     late = len(sent)
     base = (x * 2 + c) * 256
     piece = tf[rows(z * 16, 16), :]
@@ -388,9 +323,8 @@
         send(f"u{ks}{kz}", mine, mine, dev(ks=ks, kz=kz))
     drain(late)
 
-    for k in (1, 2, 3):
-        piece = wg.at[at(m, k), pl.ds(pl.multiple_of((1 - c) * 1024, 1024), 1024)]
-        recv(f"wc{k}", piece)
+    for k in (1, 3, 2):
+        recv(f"wc{k}", wpart(1 - c, 4 - k))
     for k in (1, 3, 2):
         recv(f"dy{k}", dr.at[at(m, 4 - k)])
     for j in range(4):
@@ -459,8 +393,7 @@
         vm((4, 4, ROWS, COLS), F32), vm((4, 4, ROWS, COLS), BF),
         vm((4, 3, ROWS, COLS), BF),
         vm((4, ROWS, COLS), F32), vm((4, ROWS, COLS), BF),
-        vm((112, COLS), BF), vm((96, COLS), BF), vm((112, COLS), BF), vm((96, COLS), BF),
-        vm((112, COLS), BF), vm((96, COLS), BF), vm((112, COLS), BF), vm((96, COLS), BF),
+        vm((3, ROWS, COLS), BF),
         vm((ROWS, COLS), F32), vm((8 * ROWS, COLS), BF), vm((8 * ROWS, 256), BF),
         vm((256, 8 * ROWS), BF), vm((256, COLS), F32), vm((256, COLS), BF),
         vm((15, 16, COLS), BF), vm((D, COLS), BF),

time: 82.9 us -> 87.4 us (1.054)
  Pallas kernels: 81.4 us -> 85.9 us
    pallas_call x1, Pallas kernels: 80.3 us -> 84.8 us  [per_device(): pl.pallas_call(kernel, out_shape=(jax.ShapeDtypeStruct((1, 52, D), BF), j...]
where the time goes in v4:
time: 87.4 us; the launch traced here: 87.2 us
  Pallas kernels  85.9 us (98%)
  between operations  1.31 us (1%)
    pallas_call x1, Pallas kernels, per_device(): pl.pallas_call(kernel, out_shape=(jax.ShapeDtypeStruct((1, 52, D), BF), j...  84.8 us

profile of v4, /device:TPU:1, one launch (start us, length us, event | category | flops | bytes accessed | tf_op | source)
XLA Modules:
  0.0 87.2 jit_solution(4081880600537922887)
XLA Ops:
  0.6 0.0 copy-start
  1.3 0.0 copy-done
  1.3 84.8 %shard_map.95 = (bf16[1,52,2048]{2,1,0:T(8,128)(2,1)S(1)}, bf16[2048,128]{1,0:T(8,128)(2,1)S(1)}, f32[8,128]{1,0:T(8,128)S(1)}) custom-call(s32[1]{0:T(128)S(6)} %copy.10.len_ref, s32[1,3]{1,0:T(1,128)S(1)} %copy-done, bf16[1,208,2048]{2,1,0:T(8,128)(2,1)} %hid_h.1, bf16[2048,128]{1,0:T(8,128)(2,1)} %w_h.1, bf16[1,300,1024]{2,1,0:T(8,128)(2,1)} %act_h.1, ...), custom_call_target="tpu_custom_call" | custom-call | tf_op jit(solution)/shard_map/pallas_call | solution.py:407
  86.1 1.1 %shard_map.96 = (bf16[1,52,2048]{2,1,0:T(8,128)(2,1)}, bf16[2048,128]{1,0:T(8,128)(2,1)}) custom-call(bf16[1,52,2048]{2,1,0:T(8,128)(2,1)S(1)} %get-tuple-element.5.grad_ref, bf16[2048,128]{1,0:T(8,128)(2,1)S(1)} %get-tuple-element.6.raw_ref, f32[8,128]{1,0:T(8,128)S(1)} %get-tuple-element.7.sq_ref), custom_call_target="tpu_custom_call" | custom-call | tf_op jit(solution)/shard_map/pallas_call | solution.py:422
Async XLA Ops:
  0.6 0.7 copy-start

commit v5 on v3

--- a/solution.py
+++ b/solution.py
@@ -39,9 +39,9 @@
     len_ref, view_ref, hid_h, w_h, act_h, wq_h, wakv_h, cot_h,
     o_grad, o_upd, o_sq,
     hid_v, wg, act_v, wq_v, wakv_v, cot_v, kv, akv, qs, gs, qt, gt, e_s, d_s,
-    dkv, st, yb,
-    rr, zst, za0, za1, zb0, zb1, zc0, zc1, zsc0, zsc1,
-    dres, gbuf, hx, hxt, tf, ts, zr, upd,
+    dkv, st,
+    yb, rr, zst, za0, za1, zb0, zb1, zc0, zc1,
+    dres, hid_t, ps, pc, pf, px, qx, tf, ts, zr, upd,
     sq, ysq, xs, xsq, ds, dr,
     lsem, ssem, rsem,
 ):
@@ -146,23 +146,6 @@
         send(f"zm{j}", kvp(0, j), kvp(1, j), zm)
     ysend(0)
 
-    def slot(rx, rc):
-        return pl.ds((rx * 2 + rc) * ROWS, ROWS)
-
-    def hidden_columns(kx, kc):
-        j = at(x, kx) * 2 + (1 - c if kc else c)
-        return pl.ds(pl.multiple_of(j * 256, 256), 256)
-
-    def send_hidden(kx):
-        for kc in (0, 1):
-            send(f"hx{kx}{kc}", hid_v.at[:, hidden_columns(kx, kc)],
-                 hx.at[slot(4 - kx, kc)], dev(kx=kx, kc=kc))
-
-    send_hidden(1)
-    send_hidden(3)
-    send("hx01", hid_v.at[:, hidden_columns(0, 1)], hx.at[slot(0, 1)], other)
-    hx[slot(0, 0), :] = hid_v[:, hidden_columns(0, 0)]
-
     for ref in (qs, gs):
         ref[288:304, :] = jnp.zeros((16, HD), BF)
         ref[592:608, :] = jnp.zeros((16, HD), BF)
@@ -238,7 +221,6 @@
     for i in (0, 2, 1, 3):
         recv(f"zf{i}", kvp(2, i))
     ysend(2)
-    send_hidden(2)
     ywait(3)
     attend_prefix(3)
     ywait(1)
@@ -259,80 +241,75 @@
         r0, n = HALF[h]
         return pl.ds(r0, n)
 
-    def gradients(r):
-        p = e_s[r] * (factor[r] * inverse)
-        d = p * (d_s[r] - row_dot)
+    def gradients(r, h):
+        p = e_s[r, half(h), :] * (factor[r] * inverse)
+        d = p * (d_s[r, half(h), :] - row_dot)
         dk = dot(d.astype(BF), qs[...])
         dv = dot(p.astype(BF), gs[...])
         for k in range(4):
-            half_block = (dk, dv)[k // 2][:, (k % 2) * COLS : (k % 2 + 1) * COLS]
-            dkv[r, k] = half_block
-            st[r, k] = half_block.astype(BF)
+            columns = (dk, dv)[k // 2][:, (k % 2) * COLS : (k % 2 + 1) * COLS]
+            dkv[r, k, half(h), :] = columns
+            st[r, k, half(h), :] = columns.astype(BF)
         for k in (2, 1, 3):
-            send(f"r{r}{k}", st.at[r, at(m, k)], yb.at[r, 3 - k], dev(km=k))
-
-    def finish(r):
-        piece = dkv[r, m]
+            send(f"r{r}{k}{h}", st.at[r, at(m, k), half(h)], yb.at[r, 3 - k, half(h)], dev(km=k))
+
+    def finish(r, h):
+        piece = dkv[r, m, half(h), :]
         for k in (1, 3, 2):
-            recv(f"r{r}{k}", yb.at[r, 3 - k])
-            piece = piece + yb[r, 3 - k].astype(F32)
-        rr[r] = piece
-        if r:
-            zst[r] = piece.astype(BF)
-
-    gradients(2)
-    gradients(1)
-    gradients(3)
-    gradients(0)
-    finish(2)
-    send("zap", zst.at[2, half(0)], za0, zp)
-    send("zam", zst.at[2, half(1)], za1, zm)
-    finish(1)
-    send("zbp", zst.at[1, half(1)], zb1, zp)
-    finish(3)
-    send("zbm", zst.at[3, half(0)], zb0, zm)
+            recv(f"r{r}{k}{h}", yb.at[r, 3 - k, half(h)])
+            piece = piece + yb[r, 3 - k, half(h), :].astype(F32)
+        return piece
+
+    order = ((2, 0), (2, 1), (1, 1), (3, 0), (1, 0), (3, 1))
+    for r, h in order:
+        gradients(r, h)
+    for i, (r, h) in enumerate(order[:4]):
+        zst[r, half(h), :] = finish(r, h).astype(BF)
+        target = (za0, za1, zb1, zb0)[i]
+        send(f"z{i}", zst.at[r, half(h)], target, zm if i % 2 else zp)
+        if i < 2:
+            gradients(0, i)
     early = len(sent)
-    recv("zap", za0)
-    zsc0[...] = (rr[1, half(0), :] + za0[...].astype(F32)).astype(BF)
-    send("zcp", zsc0, zc0, zp)
-    recv("zam", za1)
-    zsc1[...] = (rr[3, half(1), :] + za1[...].astype(F32)).astype(BF)
-    send("zcm", zsc1, zc1, zm)
-
-    def wpart(q, k):
-        return wg.at[at(m, k), pl.ds(pl.multiple_of(c * 1024 + q * 512, 512), 512)]
-
-    send("wp0", wpart(0, 0), wpart(0, 0), yp)
-    send("wm1", wpart(1, 0), wpart(1, 0), ym)
-    send("wp1", wpart(1, 0), wpart(1, 0), yp)
-    send("wm0", wpart(0, 0), wpart(0, 0), ym)
-
-    finish(0)
-    for kx in (1, 3, 2):
-        for kc in (0, 1):
-            recv(f"hx{kx}{kc}", hx.at[slot(4 - kx, kc)])
-    recv("hx01", hx.at[slot(0, 1)])
-    hxt[...] = hx[...].T
+    for i, (r, h), arrived, target in ((4, order[4], za0, zc0), (5, order[5], za1, zc1)):
+        piece = finish(r, h)
+        recv(f"z{i - 4}", arrived)
+        zst[r, half(h), :] = (piece + arrived[...].astype(F32)).astype(BF)
+        send(f"z{i}", zst.at[r, half(h)], target, zm if i % 2 else zp)
+
+    def wpart(half, k):
+        return wg.at[at(m, k), pl.ds(pl.multiple_of(half * 1024, 1024), 1024)]
+
+    for k in (2, 1, 3):
+        send(f"w{k}", wpart(c, 0), wpart(c, 0), dev(km=k))
+
+    for h in (0, 1):
+        rr[half(h), :] = finish(0, h)
+    hid_t[...] = hid_v[...].T
     drain(early)
 
-    def gh(rx, rc, h):
-        r0, n = HALF[h]
-        return gbuf.at[pl.ds((rx * 2 + rc) * ROWS + r0, n)]
-
-    recv("zbm", zb0)
-    recv("zcp", zc0)
-    dres[half(0), :] = rr[0, half(0), :] + zb0[...].astype(F32) + zc0[...].astype(F32)
-    gbuf[half(0), :] = dres[half(0), :].astype(BF)
+    recv("z3", zb0)
+    recv("z4", zc0)
+    dres[half(0), :] = rr[half(0), :] + zb0[...].astype(F32) + zc0[...].astype(F32)
+    recv("z2", zb1)
+    recv("z5", zc1)
+    dres[half(1), :] = rr[half(1), :] + zb1[...].astype(F32) + zc1[...].astype(F32)
+    own_grad = dres[...].astype(BF)
+
+    def rows(start, n):
+        return pl.ds(pl.multiple_of(start, n), n)
+
+    def place256(kx, kc):
+        return rows((1 - c if kc else c) * 1024 + at(x, kx) * 256, 256)
+
+    for kx in (2, 1, 3, 0):
+        ps[kx] = dot(hid_t[place256(kx, 1), :], own_grad).astype(BF)
+        send(f"p{kx}", ps.at[kx], pc.at[kx], other)
+    for kx in (2, 1, 3, 0):
+        pf[kx] = dot(hid_t[place256(kx, 0), :], own_grad)
     for kx in (2, 1, 3):
-        send(f"g{kx}0", gh(0, 0, 0), gh(4 - kx, 0, 0), dev(kx=kx))
-    send("gc00", gh(0, 0, 0), gh(0, 1, 0), other)
-    recv("zbp", zb1)
-    recv("zcm", zc1)
-    dres[half(1), :] = rr[0, half(1), :] + zb1[...].astype(F32) + zc1[...].astype(F32)
-    gbuf[half(1), :] = dres[half(1), :].astype(BF)
-    for kx in (2, 1, 3):
-        send(f"g{kx}1", gh(0, 0, 1), gh(4 - kx, 0, 1), dev(kx=kx))
-    send("gc01", gh(0, 0, 1), gh(0, 1, 1), other)
+        recv(f"p{kx}", pc.at[kx])
+        px[kx] = (pf[kx] + pc[kx].astype(F32)).astype(BF)
+        send(f"q{kx}", px.at[kx], qx.at[3 - kx], dev(kx=kx))
 
     for k in range(4):
         ds[k, 0:52, :] = dres[52 * k : 52 * k + 52, :].astype(BF)
@@ -343,41 +320,25 @@
         send(f"dy{k}", ds.at[at(m, k)], dr.at[m], dev(km=k))
     dr[m] = ds[m]
 
-    for h in (0, 1):
-        for kx in (1, 3, 2):
-            recv(f"g{kx}{h}", gh(4 - kx, 0, h))
-            send(f"gc{kx}{h}", gh(4 - kx, 0, h), gh(4 - kx, 1, h), other)
-    recv("wp0", wpart(0, 3))
-    send("wfp", wpart(0, 3), wpart(0, 3), yp)
-    recv("wm1", wpart(1, 1))
-    send("wfm", wpart(1, 1), wpart(1, 1), ym)
-    recv("gc00", gh(0, 1, 0))
-    recv("gc01", gh(0, 1, 1))
-    for h in (0, 1):
-        for kx in (1, 3, 2):
-            recv(f"gc{kx}{h}", gh(4 - kx, 1, h))
-
-    tf[...] = dot(hxt[...], gbuf[...])
-    ts[...] = tf[...].astype(BF)
-
-    def rows(start, n):
-        return pl.ds(pl.multiple_of(start, n), n)
+    recv("p0", pc.at[0])
+    part = pf[0] + pc[0].astype(F32)
+    for kx in (1, 3, 2):
+        recv(f"q{kx}", qx.at[3 - kx])
+        part = part + qx[3 - kx].astype(F32)
+
+    tf[...] = part
+    ts[...] = part.astype(BF)
 
     def place(ks, kz):
         return (at(s, ks) * 4 + at(zl, kz)) * 16
 
     for i, (ks, kz) in enumerate(along_z):
         send(f"t{ks}{kz}", ts.at[rows(place(ks, kz), 16)], zr.at[i], dev(ks=ks, kz=kz))
-    recv("wp1", wpart(1, 3))
-    recv("wm0", wpart(0, 1))
-    recv("wfp", wpart(0, 2))
-    recv("wfm", wpart(1, 2))
-    for k in (1, 2, 3):
-        piece = wg.at[at(m, k), pl.ds(pl.multiple_of(c * 1024, 1024), 1024)]
-        send(f"wc{k}", piece, piece, other)
-
+    for k in (1, 3, 2):
+        recv(f"w{k}", wpart(c, 4 - k))
+        send(f"wc{k}", wpart(c, 4 - k), wpart(c, 4 - k), other)
     late = len(sent)
-    base = (x * 2 + c) * 256
+    base = c * 1024 + x * 256
     piece = tf[rows(z * 16, 16), :]
     for i, (ks, kz) in reversed(list(enumerate(along_z))):
         recv(f"t{ks}{kz}", zr.at[i])
@@ -388,9 +349,8 @@
         send(f"u{ks}{kz}", mine, mine, dev(ks=ks, kz=kz))
     drain(late)
 
-    for k in (1, 2, 3):
-        piece = wg.at[at(m, k), pl.ds(pl.multiple_of((1 - c) * 1024, 1024), 1024)]
-        recv(f"wc{k}", piece)
+    for k in (1, 3, 2):
+        recv(f"wc{k}", wpart(1 - c, 4 - k))
     for k in (1, 3, 2):
         recv(f"dy{k}", dr.at[at(m, 4 - k)])
     for j in range(4):
@@ -399,10 +359,10 @@
         o_grad[0, :, 512 * j : 512 * j + 512] = part[:52].astype(BF)
 
     def u64(kx, ks):
-        return upd.at[rows(at(x, kx) * 512 + c * 256 + at(s, ks) * 64, 64)]
+        return upd.at[rows(c * 1024 + at(x, kx) * 256 + at(s, ks) * 64, 64)]
 
     def u256(kx, kc):
-        return upd.at[rows(at(x, kx) * 512 + (1 - c if kc else c) * 256, 256)]
+        return upd.at[place256(kx, kc)]
 
     for ks in (0, 1, 3, 2):
         for kz in (1, 2, 3, 0):
@@ -458,11 +418,12 @@
         vm((4, ROWS, QR), F32), vm((4, ROWS, QR), F32),
         vm((4, 4, ROWS, COLS), F32), vm((4, 4, ROWS, COLS), BF),
         vm((4, 3, ROWS, COLS), BF),
-        vm((4, ROWS, COLS), F32), vm((4, ROWS, COLS), BF),
+        vm((ROWS, COLS), F32), vm((4, ROWS, COLS), BF),
         vm((112, COLS), BF), vm((96, COLS), BF), vm((112, COLS), BF), vm((96, COLS), BF),
-        vm((112, COLS), BF), vm((96, COLS), BF), vm((112, COLS), BF), vm((96, COLS), BF),
-        vm((ROWS, COLS), F32), vm((8 * ROWS, COLS), BF), vm((8 * ROWS, 256), BF),
-        vm((256, 8 * ROWS), BF), vm((256, COLS), F32), vm((256, COLS), BF),
+        vm((112, COLS), BF), vm((96, COLS), BF),
+        vm((ROWS, COLS), F32), vm((D, ROWS), BF), vm((4, 256, COLS), BF), vm((4, 256, COLS), BF),
+        vm((4, 256, COLS), F32), vm((4, 256, COLS), BF), vm((3, 256, COLS), BF),
+        vm((256, COLS), F32), vm((256, COLS), BF),
         vm((15, 16, COLS), BF), vm((D, COLS), BF),
         vm((8, 128), F32), vm((3, 8, 128), F32), vm((8, 128), F32), vm((7, 8, 128), F32),
         vm((4, 64, COLS), BF), vm((4, 64, COLS), BF),

time: 82.9 us -> 84.7 us (1.022)
  Pallas kernels: 81.4 us -> 83.2 us
    pallas_call x1, Pallas kernels: 80.3 us -> 82.1 us  [per_device(): pl.pallas_call(kernel, out_shape=(jax.ShapeDtypeStruct((1, 52, D), BF), j...]
where the time goes in v5:
time: 84.7 us; the launch traced here: 84.6 us
  Pallas kernels  83.2 us (98%)
  between operations  1.31 us (2%)
    pallas_call x1, Pallas kernels, per_device(): pl.pallas_call(kernel, out_shape=(jax.ShapeDtypeStruct((1, 52, D), BF), j...  82.1 us

profile of v5, /device:TPU:1, one launch (start us, length us, event | category | flops | bytes accessed | tf_op | source)
XLA Modules:
  0.0 84.6 jit_solution(15190698180589961238)
XLA Ops:
  0.6 0.0 copy-start
  1.3 0.0 copy-done
  1.3 82.1 %shard_map.95 = (bf16[1,52,2048]{2,1,0:T(8,128)(2,1)S(1)}, bf16[2048,128]{1,0:T(8,128)(2,1)S(1)}, f32[8,128]{1,0:T(8,128)S(1)}) custom-call(s32[1]{0:T(128)S(6)} %copy.10.len_ref, s32[1,3]{1,0:T(1,128)S(1)} %copy-done, bf16[1,208,2048]{2,1,0:T(8,128)(2,1)} %hid_h.1, bf16[2048,128]{1,0:T(8,128)(2,1)} %w_h.1, bf16[1,300,1024]{2,1,0:T(8,128)(2,1)} %act_h.1, ...), custom_call_target="tpu_custom_call" | custom-call | tf_op jit(solution)/shard_map/pallas_call | solution.py:435
  83.4 1.1 %shard_map.96 = (bf16[1,52,2048]{2,1,0:T(8,128)(2,1)}, bf16[2048,128]{1,0:T(8,128)(2,1)}) custom-call(bf16[1,52,2048]{2,1,0:T(8,128)(2,1)S(1)} %get-tuple-element.5.grad_ref, bf16[2048,128]{1,0:T(8,128)(2,1)S(1)} %get-tuple-element.6.raw_ref, f32[8,128]{1,0:T(8,128)S(1)} %get-tuple-element.7.sq_ref), custom_call_target="tpu_custom_call" | custom-call | tf_op jit(solution)/shard_map/pallas_call | solution.py:450
Async XLA Ops:
  0.6 0.7 copy-start

commit v6 on v3

--- a/solution.py
+++ b/solution.py
@@ -38,7 +38,7 @@
 def kernel(
     len_ref, view_ref, hid_h, w_h, act_h, wq_h, wakv_h, cot_h,
     o_grad, o_upd, o_sq,
-    hid_v, wg, act_v, wq_v, wakv_v, cot_v, kv, akv, qs, gs, qt, gt, e_s, d_s,
+    hid_v, wg, act_v, wq_v, wakv_v, cot_v, kv, akv, qs, gs, qt, gt, e_s, d_s, bmax, bsum, bdot,
     dkv, st, yb,
     rr, zst, za0, za1, zb0, zb1, zc0, zc1, zsc0, zsc1,
     dres, gbuf, hx, hxt, tf, ts, zr, upd,
@@ -62,34 +62,46 @@
         d = at(x, kx) * 8 + at(zl, kz) * 2 + cc
         return {"dp": d, "sample": at(s, ks), "mp": at(m, km)}
 
-    along_z = [(ks, kz) for ks in (2, 1, 3, 0) for kz in (1, 2, 3, 0) if ks or kz]
+    def far_first(i):
+        return 2 - i + 3 * (i // 2) - 2 * (i // 3)
+
+    def along_z(i):
+        return far_first(i // 4), lax.rem(i + 1, 4)
+
     yp, ym = dev(km=1), dev(km=3)
     zp, zm = dev(ks=1), dev(ks=3)
-    xp, xm = dev(kx=1), dev(kx=3)
     other = dev(kc=1)
 
     index = {}
     sent = []
 
+    Y0, R0, T0, U0, FIRST = 0, 12, 24, 40, 56
+
     def number(name):
-        return index.setdefault(name, len(index))
-
-    def send(name, src, dst, device):
+        if isinstance(name, str):
+            return index.setdefault(name, FIRST + len(index))
+        return name
+
+    def remote(name, src, dst, device):
         i = number(name)
-        copy = pltpu.make_async_remote_copy(
+        return pltpu.make_async_remote_copy(
             src_ref=src, dst_ref=dst, send_sem=ssem.at[i], recv_sem=rsem.at[i],
             device_id=device, device_id_type=pl.DeviceIdType.MESH,
         )
+
+    def send(name, src, dst, device):
+        copy = remote(name, src, dst, device)
         copy.start()
-        sent.append(copy)
-
-    def recv(name, dst, device=None):
-        i = number(name)
-        pltpu.make_async_remote_copy(
-            src_ref=dst, dst_ref=dst, send_sem=ssem.at[i], recv_sem=rsem.at[i],
-            device_id=other if device is None else device,
-            device_id_type=pl.DeviceIdType.MESH,
-        ).wait_recv()
+        if isinstance(name, str):
+            sent.append(copy)
+
+    def recv(name, dst):
+        remote(name, dst, dst, other).wait_recv()
+
+    def sent_all(first, n, src):
+        @pl.loop(0, n)
+        def _(i):
+            remote(first + i, src, src, other).wait_send()
 
     def drain(n):
         for copy in sent[:n]:
@@ -109,7 +121,7 @@
         loads[i].start()
 
     barrier = pltpu.get_barrier_semaphore()
-    peers = [dev(km=k) for k in (1, 2, 3)] + [dev(ks=ks, kz=kz) for ks, kz in along_z] + [other]
+    peers = [dev(km=k) for k in (1, 2, 3)] + [dev(ks=i // 4, kz=i % 4) for i in range(1, 16)] + [other]
     peers += [dev(kx=k, kc=kc) for k in (1, 2, 3) for kc in (0, 1)]
     for peer in peers:
         pl.semaphore_signal(
@@ -123,11 +135,11 @@
     def ysend(r):
         block = kv.at[r, m]
         for k in (2, 1, 3):
-            send(f"y{r}{k}", block, block, dev(km=k))
+            send(Y0 + 3 * r + k - 1, block, block, dev(km=k))
 
     def ywait(r):
         for k in (1, 3, 2):
-            recv(f"y{r}{k}", kv.at[r, at(m, 4 - k)])
+            recv(Y0 + 3 * r + k - 1, kv.at[r, at(m, 4 - k)])
 
     loads[1].wait()
     loads[0].wait()
@@ -181,8 +193,6 @@
     qt[...] = qs[...].T
     gt[...] = gs[...].T
 
-    block_max, block_sum, block_dot = {}, {}, {}
-
     def attend(r, keys, values, mask, e_ref, d_ref):
         scores = mask(dot(keys, qt[...]))
         top = jnp.max(scores, axis=0, keepdims=True)
@@ -191,9 +201,9 @@
         if e_ref is not None:
             e_ref[...] = e
             d_ref[...] = d
-        block_max[r] = top
-        block_sum[r] = jnp.sum(e, axis=0, keepdims=True)
-        block_dot[r] = jnp.sum(e * d, axis=0, keepdims=True)
+        bmax[r] = top
+        bsum[r] = jnp.sum(e, axis=0, keepdims=True)
+        bdot[r] = jnp.sum(e * d, axis=0, keepdims=True)
 
     def draw(i):
         total = jnp.zeros_like(i)
@@ -211,7 +221,7 @@
     query_index = lax.broadcasted_iota(jnp.int32, (1, QR), 1)
     query_draw = draw(query_index - jnp.where(query_index >= ACTP, ACTP, 0))
     attend(
-        "a", akv[:, :HD], akv[:, HD:],
+        4, akv[:, :HD], akv[:, HD:],
         lambda scores: jnp.where(key_draw == query_draw, scores, NEG), None, None,
     )
 
@@ -233,34 +243,35 @@
     for i in (0, 1):
         recv(f"zm{i}", kvp(1, i))
     ysend(1)
-    ywait(0)
-    attend_prefix(0)
     for i in (0, 2, 1, 3):
         recv(f"zf{i}", kvp(2, i))
     ysend(2)
     send_hidden(2)
-    ywait(3)
-    attend_prefix(3)
-    ywait(1)
-    attend_prefix(1)
-    ywait(2)
-    attend_prefix(2)
-
-    blocks = ("a", 0, 1, 2, 3)
-    top = block_max["a"]
-    for r in (0, 1, 2, 3):
-        top = jnp.maximum(top, block_max[r])
-    factor = {r: jnp.exp(block_max[r] - top) for r in blocks}
-    total = sum(factor[r] * block_sum[r] for r in blocks)
+
+    @pl.loop(0, 4)
+    def _(i):
+        r = i + i // 2 - 2 * (i // 3)
+        ywait(r)
+        attend_prefix(r)
+
+    top = bmax[4]
+    for r in range(4):
+        top = jnp.maximum(top, bmax[r])
+    total = jnp.zeros_like(top)
+    weighted = jnp.zeros_like(top)
+    for r in range(5):
+        factor = jnp.exp(bmax[r] - top)
+        total = total + factor * bsum[r]
+        weighted = weighted + factor * bdot[r]
     inverse = 1.0 / total
-    row_dot = sum(factor[r] * block_dot[r] for r in blocks) * inverse
+    row_dot = weighted * inverse
 
     def half(h):
         r0, n = HALF[h]
         return pl.ds(r0, n)
 
     def gradients(r):
-        p = e_s[r] * (factor[r] * inverse)
+        p = e_s[r] * (jnp.exp(bmax[r] - top) * inverse)
         d = p * (d_s[r] - row_dot)
         dk = dot(d.astype(BF), qs[...])
         dv = dot(p.astype(BF), gs[...])
@@ -269,21 +280,21 @@
             dkv[r, k] = half_block
             st[r, k] = half_block.astype(BF)
         for k in (2, 1, 3):
-            send(f"r{r}{k}", st.at[r, at(m, k)], yb.at[r, 3 - k], dev(km=k))
+            send(R0 + 3 * r + k - 1, st.at[r, at(m, k)], yb.at[r, 3 - k], dev(km=k))
 
     def finish(r):
         piece = dkv[r, m]
         for k in (1, 3, 2):
-            recv(f"r{r}{k}", yb.at[r, 3 - k])
+            recv(R0 + 3 * r + k - 1, yb.at[r, 3 - k])
             piece = piece + yb[r, 3 - k].astype(F32)
         rr[r] = piece
         if r:
             zst[r] = piece.astype(BF)
 
-    gradients(2)
-    gradients(1)
-    gradients(3)
-    gradients(0)
+    @pl.loop(0, 4)
+    def _(i):
+        gradients(far_first(i))
+
     finish(2)
     send("zap", zst.at[2, half(0)], za0, zp)
     send("zam", zst.at[2, half(1)], za1, zm)
@@ -313,6 +324,8 @@
             recv(f"hx{kx}{kc}", hx.at[slot(4 - kx, kc)])
     recv("hx01", hx.at[slot(0, 1)])
     hxt[...] = hx[...].T
+    sent_all(Y0, 12, kv.at[0, 0])
+    sent_all(R0, 12, st.at[0, 0])
     drain(early)
 
     def gh(rx, rc, h):
@@ -366,8 +379,11 @@
     def place(ks, kz):
         return (at(s, ks) * 4 + at(zl, kz)) * 16
 
-    for i, (ks, kz) in enumerate(along_z):
-        send(f"t{ks}{kz}", ts.at[rows(place(ks, kz), 16)], zr.at[i], dev(ks=ks, kz=kz))
+    @pl.loop(0, 15)
+    def _(i):
+        ks, kz = along_z(i)
+        send(T0 + i, ts.at[rows(place(ks, kz), 16)], zr.at[i], dev(ks=ks, kz=kz))
+
     recv("wp1", wpart(1, 3))
     recv("wm0", wpart(0, 1))
     recv("wfp", wpart(0, 2))
@@ -378,14 +394,21 @@
 
     late = len(sent)
     base = (x * 2 + c) * 256
-    piece = tf[rows(z * 16, 16), :]
-    for i, (ks, kz) in reversed(list(enumerate(along_z))):
-        recv(f"t{ks}{kz}", zr.at[i])
-        piece = piece + zr[i].astype(F32)
+
+    def add(j, piece):
+        i = 14 - j
+        recv(T0 + i, zr.at[i])
+        return piece + zr[i].astype(F32)
+
     mine = upd.at[rows(base + z * 16, 16)]
-    mine[...] = piece.astype(BF)
-    for ks, kz in along_z:
-        send(f"u{ks}{kz}", mine, mine, dev(ks=ks, kz=kz))
+    mine[...] = lax.fori_loop(0, 15, add, tf[rows(z * 16, 16), :]).astype(BF)
+
+    @pl.loop(0, 15)
+    def _(i):
+        ks, kz = along_z(i)
+        send(U0 + i, mine, mine, dev(ks=ks, kz=kz))
+
+    sent_all(T0, 15, ts.at[0:16])
     drain(late)
 
     for k in (1, 2, 3):
@@ -404,11 +427,11 @@
     def u256(kx, kc):
         return upd.at[rows(at(x, kx) * 512 + (1 - c if kc else c) * 256, 256)]
 
-    for ks in (0, 1, 3, 2):
-        for kz in (1, 2, 3, 0):
-            if ks or kz:
-                source = rows(base + place(4 - ks, 4 - kz), 16)
-                recv(f"u{ks}{kz}", upd.at[source])
+    for q in (3, 1, 2, 0):
+        ks = far_first(q)
+        for i in range(4 * q, min(4 * q + 4, 15)):
+            source = rows(base + place(4 - ks, 4 - (i + 1) % 4), 16)
+            recv(U0 + i, upd.at[source])
         for kx in (2, 1, 3):
             send(f"ux{kx}{ks}", u64(0, 4 - ks), u64(0, 4 - ks), dev(kx=kx))
     send("uc0", u256(0, 0), u256(0, 0), other)
@@ -432,6 +455,7 @@
         recv(f"sx{kx}{kc}", xsq.at[i])
         everything = everything + xsq[i]
     o_sq[...] = everything
+    sent_all(U0, 15, mine)
     drain(len(sent) - 3)
     recv("uc0", u256(0, 1))
     for kx in (1, 3, 2):
@@ -456,6 +480,7 @@
         vm((1024, 512), BF), vm((ACT, 512), BF), vm((4, 4, ROWS, COLS), BF), vm((ACTP, 512), BF),
         vm((QR, HD), BF), vm((QR, HD), BF), vm((HD, QR), BF), vm((HD, QR), BF),
         vm((4, ROWS, QR), F32), vm((4, ROWS, QR), F32),
+        vm((5, 1, QR), F32), vm((5, 1, QR), F32), vm((5, 1, QR), F32),
         vm((4, 4, ROWS, COLS), F32), vm((4, 4, ROWS, COLS), BF),
         vm((4, 3, ROWS, COLS), BF),
         vm((4, ROWS, COLS), F32), vm((4, ROWS, COLS), BF),

time: 82.9 us -> 83.5 us (level)
  no operation moved by 1% of the time
where the time goes in v6:
time: 83.5 us; the launch traced here: 83.4 us
  Pallas kernels  82 us (98%)
  between operations  1.31 us (2%)
    pallas_call x1, Pallas kernels, per_device(): pl.pallas_call(kernel, out_shape=(jax.ShapeDtypeStruct((1, 52, D), BF), j...  80.9 us

profile of v6, /device:TPU:1, one launch (start us, length us, event | category | flops | bytes accessed | tf_op | source)
XLA Modules:
  0.0 83.4 jit_solution(9490604153691286767)
XLA Ops:
  0.6 0.0 copy-start
  1.3 0.0 copy-done
  1.3 80.9 %shard_map.95 = (bf16[1,52,2048]{2,1,0:T(8,128)(2,1)S(1)}, bf16[2048,128]{1,0:T(8,128)(2,1)S(1)}, f32[8,128]{1,0:T(8,128)S(1)}) custom-call(s32[1]{0:T(128)S(6)} %copy.10.len_ref, s32[1,3]{1,0:T(1,128)S(1)} %copy-done, bf16[1,208,2048]{2,1,0:T(8,128)(2,1)} %hid_h.1, bf16[2048,128]{1,0:T(8,128)(2,1)} %w_h.1, bf16[1,300,1024]{2,1,0:T(8,128)(2,1)} %act_h.1, ...), custom_call_target="tpu_custom_call" | custom-call | tf_op jit(solution)/shard_map/pallas_call | solution.py:499
  82.3 1.1 %shard_map.96 = (bf16[1,52,2048]{2,1,0:T(8,128)(2,1)}, bf16[2048,128]{1,0:T(8,128)(2,1)}) custom-call(bf16[1,52,2048]{2,1,0:T(8,128)(2,1)S(1)} %get-tuple-element.5.grad_ref, bf16[2048,128]{1,0:T(8,128)(2,1)S(1)} %get-tuple-element.6.raw_ref, f32[8,128]{1,0:T(8,128)S(1)} %get-tuple-element.7.sq_ref), custom_call_target="tpu_custom_call" | custom-call | tf_op jit(solution)/shard_map/pallas_call | solution.py:514
Async XLA Ops:
  0.6 0.7 copy-start

commit v7 on v5

--- a/solution.py
+++ b/solution.py
@@ -39,9 +39,9 @@
     len_ref, view_ref, hid_h, w_h, act_h, wq_h, wakv_h, cot_h,
     o_grad, o_upd, o_sq,
     hid_v, wg, act_v, wq_v, wakv_v, cot_v, kv, akv, qs, gs, qt, gt, e_s, d_s,
-    dkv, st,
-    yb, rr, zst, za0, za1, zb0, zb1, zc0, zc1,
-    dres, hid_t, ps, pc, pf, px, qx, tf, ts, zr, upd,
+    dkv, st, yb,
+    rr, zst, za0, za1, zb0, zb1, zc0, zc1,
+    dres, gbuf, hx, hxt, tf, ts, zr, upd,
     sq, ysq, xs, xsq, ds, dr,
     lsem, ssem, rsem,
 ):
@@ -63,9 +63,7 @@
         return {"dp": d, "sample": at(s, ks), "mp": at(m, km)}
 
     along_z = [(ks, kz) for ks in (2, 1, 3, 0) for kz in (1, 2, 3, 0) if ks or kz]
-    yp, ym = dev(km=1), dev(km=3)
     zp, zm = dev(ks=1), dev(ks=3)
-    xp, xm = dev(kx=1), dev(kx=3)
     other = dev(kc=1)
 
     index = {}
@@ -146,6 +144,23 @@
         send(f"zm{j}", kvp(0, j), kvp(1, j), zm)
     ysend(0)
 
+    def slot(rx, rc):
+        return pl.ds((rx * 2 + rc) * ROWS, ROWS)
+
+    def hidden_columns(kx, kc):
+        j = at(x, kx) * 2 + (1 - c if kc else c)
+        return pl.ds(pl.multiple_of(j * 256, 256), 256)
+
+    def send_hidden(kx):
+        for kc in (0, 1):
+            send(f"hx{kx}{kc}", hid_v.at[:, hidden_columns(kx, kc)],
+                 hx.at[slot(4 - kx, kc)], dev(kx=kx, kc=kc))
+
+    send_hidden(1)
+    send_hidden(3)
+    send("hx01", hid_v.at[:, hidden_columns(0, 1)], hx.at[slot(0, 1)], other)
+    hx[slot(0, 0), :] = hid_v[:, hidden_columns(0, 0)]
+
     for ref in (qs, gs):
         ref[288:304, :] = jnp.zeros((16, HD), BF)
         ref[592:608, :] = jnp.zeros((16, HD), BF)
@@ -221,6 +236,7 @@
     for i in (0, 2, 1, 3):
         recv(f"zf{i}", kvp(2, i))
     ysend(2)
+    send_hidden(2)
     ywait(3)
     attend_prefix(3)
     ywait(1)
@@ -276,16 +292,23 @@
         zst[r, half(h), :] = (piece + arrived[...].astype(F32)).astype(BF)
         send(f"z{i}", zst.at[r, half(h)], target, zm if i % 2 else zp)
 
-    def wpart(half, k):
-        return wg.at[at(m, k), pl.ds(pl.multiple_of(half * 1024, 1024), 1024)]
+    def wpart(part, k):
+        return wg.at[at(m, k), pl.ds(pl.multiple_of(part * 1024, 1024), 1024)]
 
     for k in (2, 1, 3):
         send(f"w{k}", wpart(c, 0), wpart(c, 0), dev(km=k))
 
     for h in (0, 1):
         rr[half(h), :] = finish(0, h)
-    hid_t[...] = hid_v[...].T
+    for kx in (1, 3, 2):
+        for kc in (0, 1):
+            recv(f"hx{kx}{kc}", hx.at[slot(4 - kx, kc)])
+    recv("hx01", hx.at[slot(0, 1)])
+    hxt[...] = hx[...].T
     drain(early)
+
+    def block(rx, rc):
+        return gbuf.at[slot(rx, rc)]
 
     recv("z3", zb0)
     recv("z4", zc0)
@@ -293,23 +316,10 @@
     recv("z2", zb1)
     recv("z5", zc1)
     dres[half(1), :] = rr[half(1), :] + zb1[...].astype(F32) + zc1[...].astype(F32)
-    own_grad = dres[...].astype(BF)
-
-    def rows(start, n):
-        return pl.ds(pl.multiple_of(start, n), n)
-
-    def place256(kx, kc):
-        return rows((1 - c if kc else c) * 1024 + at(x, kx) * 256, 256)
-
-    for kx in (2, 1, 3, 0):
-        ps[kx] = dot(hid_t[place256(kx, 1), :], own_grad).astype(BF)
-        send(f"p{kx}", ps.at[kx], pc.at[kx], other)
-    for kx in (2, 1, 3, 0):
-        pf[kx] = dot(hid_t[place256(kx, 0), :], own_grad)
+    gbuf[slot(0, 0), :] = dres[...].astype(BF)
     for kx in (2, 1, 3):
-        recv(f"p{kx}", pc.at[kx])
-        px[kx] = (pf[kx] + pc[kx].astype(F32)).astype(BF)
-        send(f"q{kx}", px.at[kx], qx.at[3 - kx], dev(kx=kx))
+        send(f"g{kx}", block(0, 0), block(4 - kx, 0), dev(kx=kx))
+    send("gc0", block(0, 0), block(0, 1), other)
 
     for k in range(4):
         ds[k, 0:52, :] = dres[52 * k : 52 * k + 52, :].astype(BF)
@@ -320,14 +330,17 @@
         send(f"dy{k}", ds.at[at(m, k)], dr.at[m], dev(km=k))
     dr[m] = ds[m]
 
-    recv("p0", pc.at[0])
-    part = pf[0] + pc[0].astype(F32)
     for kx in (1, 3, 2):
-        recv(f"q{kx}", qx.at[3 - kx])
-        part = part + qx[3 - kx].astype(F32)
-
-    tf[...] = part
-    ts[...] = part.astype(BF)
+        recv(f"g{kx}", block(4 - kx, 0))
+        send(f"gc{kx}", block(4 - kx, 0), block(4 - kx, 1), other)
+    for kx in (0, 1, 3, 2):
+        recv(f"gc{kx}", block((4 - kx) % 4, 1))
+
+    tf[...] = dot(hxt[...], gbuf[...])
+    ts[...] = tf[...].astype(BF)
+
+    def rows(start, n):
+        return pl.ds(pl.multiple_of(start, n), n)
 
     def place(ks, kz):
         return (at(s, ks) * 4 + at(zl, kz)) * 16
@@ -338,7 +351,7 @@
         recv(f"w{k}", wpart(c, 4 - k))
         send(f"wc{k}", wpart(c, 4 - k), wpart(c, 4 - k), other)
     late = len(sent)
-    base = c * 1024 + x * 256
+    base = (x * 2 + c) * 256
     piece = tf[rows(z * 16, 16), :]
     for i, (ks, kz) in reversed(list(enumerate(along_z))):
         recv(f"t{ks}{kz}", zr.at[i])
@@ -359,10 +372,10 @@
         o_grad[0, :, 512 * j : 512 * j + 512] = part[:52].astype(BF)
 
     def u64(kx, ks):
-        return upd.at[rows(c * 1024 + at(x, kx) * 256 + at(s, ks) * 64, 64)]
+        return upd.at[rows(at(x, kx) * 512 + c * 256 + at(s, ks) * 64, 64)]
 
     def u256(kx, kc):
-        return upd.at[place256(kx, kc)]
+        return upd.at[rows(at(x, kx) * 512 + (1 - c if kc else c) * 256, 256)]
 
     for ks in (0, 1, 3, 2):
         for kz in (1, 2, 3, 0):
@@ -421,9 +434,8 @@
         vm((ROWS, COLS), F32), vm((4, ROWS, COLS), BF),
         vm((112, COLS), BF), vm((96, COLS), BF), vm((112, COLS), BF), vm((96, COLS), BF),
         vm((112, COLS), BF), vm((96, COLS), BF),
-        vm((ROWS, COLS), F32), vm((D, ROWS), BF), vm((4, 256, COLS), BF), vm((4, 256, COLS), BF),
-        vm((4, 256, COLS), F32), vm((4, 256, COLS), BF), vm((3, 256, COLS), BF),
-        vm((256, COLS), F32), vm((256, COLS), BF),
+        vm((ROWS, COLS), F32), vm((8 * ROWS, COLS), BF), vm((8 * ROWS, 256), BF),
+        vm((256, 8 * ROWS), BF), vm((256, COLS), F32), vm((256, COLS), BF),
         vm((15, 16, COLS), BF), vm((D, COLS), BF),
         vm((8, 128), F32), vm((3, 8, 128), F32), vm((8, 128), F32), vm((7, 8, 128), F32),
         vm((4, 64, COLS), BF), vm((4, 64, COLS), BF),

time: 84.7 us -> 83.8 us (0.989)
  Pallas kernels: 83.2 us -> 82.3 us
    pallas_call x1, Pallas kernels: 82.1 us -> 81.2 us  [per_device(): pl.pallas_call(kernel, out_shape=(jax.ShapeDtypeStruct((1, 52, D), BF), j...]
where the time goes in v7:
time: 83.8 us; the launch traced here: 83.6 us
  Pallas kernels  82.3 us (98%)
  between operations  1.31 us (2%)
    pallas_call x1, Pallas kernels, per_device(): pl.pallas_call(kernel, out_shape=(jax.ShapeDtypeStruct((1, 52, D), BF), j...  81.2 us

profile of v7, /device:TPU:1, one launch (start us, length us, event | category | flops | bytes accessed | tf_op | source)
XLA Modules:
  0.0 83.6 jit_solution(17143382222754599268)
XLA Ops:
  0.6 0.0 copy-start
  1.3 0.0 copy-done
  1.3 81.2 %shard_map.95 = (bf16[1,52,2048]{2,1,0:T(8,128)(2,1)S(1)}, bf16[2048,128]{1,0:T(8,128)(2,1)S(1)}, f32[8,128]{1,0:T(8,128)S(1)}) custom-call(s32[1]{0:T(128)S(6)} %copy.10.len_ref, s32[1,3]{1,0:T(1,128)S(1)} %copy-done, bf16[1,208,2048]{2,1,0:T(8,128)(2,1)} %hid_h.1, bf16[2048,128]{1,0:T(8,128)(2,1)} %w_h.1, bf16[1,300,1024]{2,1,0:T(8,128)(2,1)} %act_h.1, ...), custom_call_target="tpu_custom_call" | custom-call | tf_op jit(solution)/shard_map/pallas_call | solution.py:447
  82.5 1.1 %shard_map.96 = (bf16[1,52,2048]{2,1,0:T(8,128)(2,1)}, bf16[2048,128]{1,0:T(8,128)(2,1)}) custom-call(bf16[1,52,2048]{2,1,0:T(8,128)(2,1)S(1)} %get-tuple-element.5.grad_ref, bf16[2048,128]{1,0:T(8,128)(2,1)S(1)} %get-tuple-element.6.raw_ref, f32[8,128]{1,0:T(8,128)S(1)} %get-tuple-element.7.sq_ref), custom_call_target="tpu_custom_call" | custom-call | tf_op jit(solution)/shard_map/pallas_call | solution.py:462
Async XLA Ops:
  0.6 0.7 copy-start

commit v8 on v3

--- a/solution.py
+++ b/solution.py
@@ -36,14 +36,14 @@
 
 
 def kernel(
-    len_ref, view_ref, hid_h, w_h, act_h, wq_h, wakv_h, cot_h,
+    len_ref, view_h, hid_h, w_h, act_h, wq_h, wakv_h, cot_h,
     o_grad, o_upd, o_sq,
     hid_v, wg, act_v, wq_v, wakv_v, cot_v, kv, akv, qs, gs, qt, gt, e_s, d_s,
-    dkv, st, yb,
+    dkv, st, ya0, ya1, yb0, yb1, yc0, yc1, sc0, sc1,
     rr, zst, za0, za1, zb0, zb1, zc0, zc1, zsc0, zsc1,
     dres, gbuf, hx, hxt, tf, ts, zr, upd,
     sq, ysq, xs, xsq, ds, dr,
-    lsem, ssem, rsem,
+    view_ref, lsem, ssem, rsem,
 ):
     dp = lax.axis_index("dp")
     s = lax.axis_index("sample")
@@ -105,7 +105,8 @@
         pltpu.make_async_copy(cot_h.at[0], cot_v, lsem.at[5]),
         pltpu.make_async_copy(hid_h.at[0, 112:208], hid_v.at[112:208], lsem.at[6]),
     ]
-    for i in (1, 0, 6):
+    loads.append(pltpu.make_async_copy(view_h, view_ref, lsem.at[7]))
+    for i in (1, 0, 6, 7):
         loads[i].start()
 
     barrier = pltpu.get_barrier_semaphore()
@@ -214,6 +215,8 @@
         "a", akv[:, :HD], akv[:, HD:],
         lambda scores: jnp.where(key_draw == query_draw, scores, NEG), None, None,
     )
+
+    loads[7].wait()
 
     def attend_prefix(r):
         p = at(s, r) * ROWS + lax.broadcasted_iota(jnp.int32, (ROWS, 1), 0)
@@ -268,27 +271,42 @@
             half_block = (dk, dv)[k // 2][:, (k % 2) * COLS : (k % 2 + 1) * COLS]
             dkv[r, k] = half_block
             st[r, k] = half_block.astype(BF)
-        for k in (2, 1, 3):
-            send(f"r{r}{k}", st.at[r, at(m, k)], yb.at[r, 3 - k], dev(km=k))
+        send(f"ra{r}p", st.at[r, at(m, 2), half(0)], ya0.at[r], yp)
+        send(f"ra{r}m", st.at[r, at(m, 2), half(1)], ya1.at[r], ym)
+        send(f"rb{r}p", st.at[r, at(m, 1), half(1)], yb1.at[r], yp)
+        send(f"rb{r}m", st.at[r, at(m, 3), half(0)], yb0.at[r], ym)
+
+    def combine(r):
+        recv(f"ra{r}p", ya0.at[r])
+        sc0[r] = (dkv[r, at(m, 1), half(0), :] + ya0[r].astype(F32)).astype(BF)
+        send(f"rc{r}p", sc0.at[r], yc0.at[r], yp)
+        recv(f"ra{r}m", ya1.at[r])
+        sc1[r] = (dkv[r, at(m, 3), half(1), :] + ya1[r].astype(F32)).astype(BF)
+        send(f"rc{r}m", sc1.at[r], yc1.at[r], ym)
 
     def finish(r):
-        piece = dkv[r, m]
-        for k in (1, 3, 2):
-            recv(f"r{r}{k}", yb.at[r, 3 - k])
-            piece = piece + yb[r, 3 - k].astype(F32)
-        rr[r] = piece
+        recv(f"rb{r}m", yb0.at[r])
+        recv(f"rc{r}p", yc0.at[r])
+        rr[r, half(0), :] = dkv[r, m, half(0), :] + yb0[r].astype(F32) + yc0[r].astype(F32)
+        recv(f"rb{r}p", yb1.at[r])
+        recv(f"rc{r}m", yc1.at[r])
+        rr[r, half(1), :] = dkv[r, m, half(1), :] + yb1[r].astype(F32) + yc1[r].astype(F32)
         if r:
-            zst[r] = piece.astype(BF)
+            zst[r] = rr[r].astype(BF)
 
     gradients(2)
     gradients(1)
+    combine(2)
     gradients(3)
+    combine(1)
     gradients(0)
+    combine(3)
     finish(2)
     send("zap", zst.at[2, half(0)], za0, zp)
     send("zam", zst.at[2, half(1)], za1, zm)
     finish(1)
     send("zbp", zst.at[1, half(1)], zb1, zp)
+    combine(0)
     finish(3)
     send("zbm", zst.at[3, half(0)], zb0, zm)
     early = len(sent)
@@ -457,7 +475,9 @@
         vm((QR, HD), BF), vm((QR, HD), BF), vm((HD, QR), BF), vm((HD, QR), BF),
         vm((4, ROWS, QR), F32), vm((4, ROWS, QR), F32),
         vm((4, 4, ROWS, COLS), F32), vm((4, 4, ROWS, COLS), BF),
-        vm((4, 3, ROWS, COLS), BF),
+        vm((4, 112, COLS), BF), vm((4, 96, COLS), BF), vm((4, 112, COLS), BF),
+        vm((4, 96, COLS), BF), vm((4, 112, COLS), BF), vm((4, 96, COLS), BF),
+        vm((4, 112, COLS), BF), vm((4, 96, COLS), BF),
         vm((4, ROWS, COLS), F32), vm((4, ROWS, COLS), BF),
         vm((112, COLS), BF), vm((96, COLS), BF), vm((112, COLS), BF), vm((96, COLS), BF),
         vm((112, COLS), BF), vm((96, COLS), BF), vm((112, COLS), BF), vm((96, COLS), BF),
@@ -466,7 +486,8 @@
         vm((15, 16, COLS), BF), vm((D, COLS), BF),
         vm((8, 128), F32), vm((3, 8, 128), F32), vm((8, 128), F32), vm((7, 8, 128), F32),
         vm((4, 64, COLS), BF), vm((4, 64, COLS), BF),
-        pltpu.SemaphoreType.DMA((7,)),
+        pltpu.SMEM((1, VIEWS), jnp.int32),
+        pltpu.SemaphoreType.DMA((8,)),
         pltpu.SemaphoreType.DMA((N_SEMS,)), pltpu.SemaphoreType.DMA((N_SEMS,)),
     ]
     smem = pl.BlockSpec(memory_space=pltpu.SMEM)
@@ -478,14 +499,14 @@
             jax.ShapeDtypeStruct((D, COLS), BF),
             jax.ShapeDtypeStruct((8, 128), F32),
         ),
-        in_specs=[smem, smem] + [hbm] * 6,
+        in_specs=[smem] + [hbm] * 7,
         out_specs=(pl.BlockSpec(memory_space=pltpu.VMEM),) * 3,
         scratch_shapes=scratch,
         compiler_params=pltpu.CompilerParams(
             collective_id=0, has_side_effects=True, vmem_limit_bytes=40 * 1024 * 1024
         ),
     )(
-        prompt_len, view_valid, *[pltpu.with_memory_space_constraint(v, pltpu.HBM) for v in (prefix_hidden, prefix_kv_weight, action_hidden, query_weight, action_kv_weight, out_cotangent)])
+        prompt_len, *[pltpu.with_memory_space_constraint(v, pltpu.HBM) for v in (view_valid, prefix_hidden, prefix_kv_weight, action_hidden, query_weight, action_kv_weight, out_cotangent)])
     return pl.pallas_call(
         write_results,
         out_shape=(

time: 82.9 us -> 85.3 us (1.029)
  Pallas kernels: 81.4 us -> 83.8 us
    pallas_call x1, Pallas kernels: 80.3 us -> 82.7 us  [per_device(): pl.pallas_call(kernel, out_shape=(jax.ShapeDtypeStruct((1, 52, D), BF), j...]
where the time goes in v8:
time: 85.3 us; the launch traced here: 85.1 us
  Pallas kernels  83.8 us (98%)
  between operations  1.29 us (2%)
    pallas_call x1, Pallas kernels, per_device(): pl.pallas_call(kernel, out_shape=(jax.ShapeDtypeStruct((1, 52, D), BF), j...  82.7 us

profile of v8, /device:TPU:1, one launch (start us, length us, event | category | flops | bytes accessed | tf_op | source)
XLA Modules:
  0.0 85.1 jit_solution(1341563512748169545)
XLA Ops:
  1.3 82.7 %shard_map.95 = (bf16[1,52,2048]{2,1,0:T(8,128)(2,1)S(1)}, bf16[2048,128]{1,0:T(8,128)(2,1)S(1)}, f32[8,128]{1,0:T(8,128)S(1)}) custom-call(s32[1]{0:T(128)S(6)} %copy.10.len_ref, s32[1,3]{1,0:T(1,128)} %view_h.1, bf16[1,208,2048]{2,1,0:T(8,128)(2,1)} %hid_h.1, bf16[2048,128]{1,0:T(8,128)(2,1)} %w_h.1, bf16[1,300,1024]{2,1,0:T(8,128)(2,1)} %act_h.1, ...), custom_call_target="tpu_custom_call" | custom-call | tf_op jit(solution)/shard_map/pallas_call | solution.py:495
  84.0 1.1 %shard_map.96 = (bf16[1,52,2048]{2,1,0:T(8,128)(2,1)}, bf16[2048,128]{1,0:T(8,128)(2,1)}) custom-call(bf16[1,52,2048]{2,1,0:T(8,128)(2,1)S(1)} %get-tuple-element.5.grad_ref, bf16[2048,128]{1,0:T(8,128)(2,1)S(1)} %get-tuple-element.6.raw_ref, f32[8,128]{1,0:T(8,128)S(1)} %get-tuple-element.7.sq_ref), custom_call_target="tpu_custom_call" | custom-call | tf_op jit(solution)/shard_map/pallas_call | solution.py:510

commit v9 on v7

--- a/solution.py
+++ b/solution.py
@@ -36,14 +36,14 @@
 
 
 def kernel(
-    len_ref, view_ref, hid_h, w_h, act_h, wq_h, wakv_h, cot_h,
+    len_ref, view_h, hid_h, w_h, act_h, wq_h, wakv_h, cot_h,
     o_grad, o_upd, o_sq,
     hid_v, wg, act_v, wq_v, wakv_v, cot_v, kv, akv, qs, gs, qt, gt, e_s, d_s,
     dkv, st, yb,
     rr, zst, za0, za1, zb0, zb1, zc0, zc1,
     dres, gbuf, hx, hxt, tf, ts, zr, upd,
     sq, ysq, xs, xsq, ds, dr,
-    lsem, ssem, rsem,
+    view_ref, lsem, ssem, rsem,
 ):
     dp = lax.axis_index("dp")
     s = lax.axis_index("sample")
@@ -103,7 +103,8 @@
         pltpu.make_async_copy(cot_h.at[0], cot_v, lsem.at[5]),
         pltpu.make_async_copy(hid_h.at[0, 112:208], hid_v.at[112:208], lsem.at[6]),
     ]
-    for i in (1, 0, 6):
+    loads.append(pltpu.make_async_copy(view_h, view_ref, lsem.at[7]))
+    for i in (1, 0, 6, 7):
         loads[i].start()
 
     barrier = pltpu.get_barrier_semaphore()
@@ -118,14 +119,17 @@
         r0, n = PART[i]
         return kv.at[r, m, pl.ds(r0, n)]
 
-    def ysend(r):
-        block = kv.at[r, m]
+    def ysend(r, h):
+        r0, n = HALF[h]
+        block = kv.at[r, m, pl.ds(r0, n)]
         for k in (2, 1, 3):
-            send(f"y{r}{k}", block, block, dev(km=k))
+            send(f"y{r}{k}{h}", block, block, dev(km=k))
 
     def ywait(r):
-        for k in (1, 3, 2):
-            recv(f"y{r}{k}", kv.at[r, at(m, 4 - k)])
+        for h in (0, 1):
+            r0, n = HALF[h]
+            for k in (1, 3, 2):
+                recv(f"y{r}{k}{h}", kv.at[r, at(m, 4 - k), pl.ds(r0, n)])
 
     loads[1].wait()
     loads[0].wait()
@@ -142,7 +146,8 @@
     for i, j in ((2, 0), (3, 1)):
         send(f"zp{i}", kvp(0, i), kvp(3, i), zp)
         send(f"zm{j}", kvp(0, j), kvp(1, j), zm)
-    ysend(0)
+    ysend(0, 0)
+    ysend(0, 1)
 
     def slot(rx, rc):
         return pl.ds((rx * 2 + rc) * ROWS, ROWS)
@@ -204,6 +209,8 @@
         send(f"zf{i}", kvp(3, i), kvp(2, i), zp)
         recv(f"zm{j}", kvp(1, j))
         send(f"zf{j}", kvp(1, j), kvp(2, j), zm)
+    ysend(3, 0)
+    ysend(1, 1)
 
     key_draw = draw(lax.broadcasted_iota(jnp.int32, (ACTP, 1), 0))
     query_index = lax.broadcasted_iota(jnp.int32, (1, QR), 1)
@@ -212,6 +219,8 @@
         "a", akv[:, :HD], akv[:, HD:],
         lambda scores: jnp.where(key_draw == query_draw, scores, NEG), None, None,
     )
+
+    loads[7].wait()
 
     def attend_prefix(r):
         p = at(s, r) * ROWS + lax.broadcasted_iota(jnp.int32, (ROWS, 1), 0)
@@ -227,15 +236,18 @@
 
     for i in (2, 3):
         recv(f"zp{i}", kvp(3, i))
-    ysend(3)
+    ysend(3, 1)
     for i in (0, 1):
         recv(f"zm{i}", kvp(1, i))
-    ysend(1)
+    ysend(1, 0)
     ywait(0)
     attend_prefix(0)
-    for i in (0, 2, 1, 3):
+    for i in (0, 1):
         recv(f"zf{i}", kvp(2, i))
-    ysend(2)
+    ysend(2, 0)
+    for i in (2, 3):
+        recv(f"zf{i}", kvp(2, i))
+    ysend(2, 1)
     send_hidden(2)
     ywait(3)
     attend_prefix(3)
@@ -439,7 +451,8 @@
         vm((15, 16, COLS), BF), vm((D, COLS), BF),
         vm((8, 128), F32), vm((3, 8, 128), F32), vm((8, 128), F32), vm((7, 8, 128), F32),
         vm((4, 64, COLS), BF), vm((4, 64, COLS), BF),
-        pltpu.SemaphoreType.DMA((7,)),
+        pltpu.SMEM((1, VIEWS), jnp.int32),
+        pltpu.SemaphoreType.DMA((8,)),
         pltpu.SemaphoreType.DMA((N_SEMS,)), pltpu.SemaphoreType.DMA((N_SEMS,)),
     ]
     smem = pl.BlockSpec(memory_space=pltpu.SMEM)
@@ -451,14 +464,14 @@
             jax.ShapeDtypeStruct((D, COLS), BF),
             jax.ShapeDtypeStruct((8, 128), F32),
         ),
-        in_specs=[smem, smem] + [hbm] * 6,
+        in_specs=[smem] + [hbm] * 7,
         out_specs=(pl.BlockSpec(memory_space=pltpu.VMEM),) * 3,
         scratch_shapes=scratch,
         compiler_params=pltpu.CompilerParams(
             collective_id=0, has_side_effects=True, vmem_limit_bytes=40 * 1024 * 1024
         ),
     )(
-        prompt_len, view_valid, *[pltpu.with_memory_space_constraint(v, pltpu.HBM) for v in (prefix_hidden, prefix_kv_weight, action_hidden, query_weight, action_kv_weight, out_cotangent)])
+        prompt_len, *[pltpu.with_memory_space_constraint(v, pltpu.HBM) for v in (view_valid, prefix_hidden, prefix_kv_weight, action_hidden, query_weight, action_kv_weight, out_cotangent)])
     return pl.pallas_call(
         write_results,
         out_shape=(

time: 83.8 us -> 82.8 us (0.988)
  Pallas kernels: 82.3 us -> 81.4 us
    pallas_call x1, Pallas kernels: 81.2 us -> 80.3 us  [per_device(): pl.pallas_call(kernel, out_shape=(jax.ShapeDtypeStruct((1, 52, D), BF), j...]
where the time goes in v9:
time: 82.8 us; the launch traced here: 82.7 us
  Pallas kernels  81.4 us (98%)
  between operations  1.29 us (2%)
    pallas_call x1, Pallas kernels, per_device(): pl.pallas_call(kernel, out_shape=(jax.ShapeDtypeStruct((1, 52, D), BF), j...  80.3 us

profile of v9, /device:TPU:1, one launch (start us, length us, event | category | flops | bytes accessed | tf_op | source)
XLA Modules:
  0.0 82.7 jit_solution(8677013566487712238)
XLA Ops:
  1.3 80.3 %shard_map.95 = (bf16[1,52,2048]{2,1,0:T(8,128)(2,1)S(1)}, bf16[2048,128]{1,0:T(8,128)(2,1)S(1)}, f32[8,128]{1,0:T(8,128)S(1)}) custom-call(s32[1]{0:T(128)S(6)} %copy.10.len_ref, s32[1,3]{1,0:T(1,128)} %view_h.1, bf16[1,208,2048]{2,1,0:T(8,128)(2,1)} %hid_h.1, bf16[2048,128]{1,0:T(8,128)(2,1)} %w_h.1, bf16[1,300,1024]{2,1,0:T(8,128)(2,1)} %act_h.1, ...), custom_call_target="tpu_custom_call" | custom-call | tf_op jit(solution)/shard_map/pallas_call | solution.py:460
  81.6 1.1 %shard_map.96 = (bf16[1,52,2048]{2,1,0:T(8,128)(2,1)}, bf16[2048,128]{1,0:T(8,128)(2,1)}) custom-call(bf16[1,52,2048]{2,1,0:T(8,128)(2,1)S(1)} %get-tuple-element.5.grad_ref, bf16[2048,128]{1,0:T(8,128)(2,1)S(1)} %get-tuple-element.6.raw_ref, f32[8,128]{1,0:T(8,128)S(1)} %get-tuple-element.7.sq_ref), custom_call_target="tpu_custom_call" | custom-call | tf_op jit(solution)/shard_map/pallas_call | solution.py:475

commit v10 on v9

--- a/solution.py
+++ b/solution.py
@@ -20,7 +20,7 @@
 NEG = -3.0e38
 HALF = ((0, 112), (112, 96))
 PART = ((0, 64), (64, 48), (112, 48), (160, 48))
-N_SEMS = 160
+N_SEMS = 200
 
 
 def dot(a, b):
@@ -41,7 +41,7 @@
     hid_v, wg, act_v, wq_v, wakv_v, cot_v, kv, akv, qs, gs, qt, gt, e_s, d_s,
     dkv, st, yb,
     rr, zst, za0, za1, zb0, zb1, zc0, zc1,
-    dres, gbuf, hx, hxt, tf, ts, zr, upd,
+    dres, gbuf, hx, hxa, hxb, tf, ts, zr, upd,
     sq, ysq, xs, xsq, ds, dr,
     view_ref, lsem, ssem, rsem,
 ):
@@ -150,7 +150,7 @@
     ysend(0, 1)
 
     def slot(rx, rc):
-        return pl.ds((rx * 2 + rc) * ROWS, ROWS)
+        return pl.ds((rc * 4 + rx) * ROWS, ROWS)
 
     def hidden_columns(kx, kc):
         j = at(x, kx) * 2 + (1 - c if kc else c)
@@ -316,7 +316,8 @@
         for kc in (0, 1):
             recv(f"hx{kx}{kc}", hx.at[slot(4 - kx, kc)])
     recv("hx01", hx.at[slot(0, 1)])
-    hxt[...] = hx[...].T
+    hxa[...] = hx[0 : 4 * ROWS, :].T
+    hxb[...] = hx[4 * ROWS : 8 * ROWS, :].T
     drain(early)
 
     def block(rx, rc):
@@ -345,11 +346,13 @@
     for kx in (1, 3, 2):
         recv(f"g{kx}", block(4 - kx, 0))
         send(f"gc{kx}", block(4 - kx, 0), block(4 - kx, 1), other)
+    tf[...] = dot(hxa[...], gbuf[0 : 4 * ROWS, :])
     for kx in (0, 1, 3, 2):
         recv(f"gc{kx}", block((4 - kx) % 4, 1))
 
-    tf[...] = dot(hxt[...], gbuf[...])
-    ts[...] = tf[...].astype(BF)
+    part = tf[...] + dot(hxb[...], gbuf[4 * ROWS : 8 * ROWS, :])
+    tf[...] = part
+    ts[...] = part.astype(BF)
 
     def rows(start, n):
         return pl.ds(pl.multiple_of(start, n), n)
@@ -383,20 +386,19 @@
         part = dot_nt(wide(dr[0], dr[1], dr[2], dr[3]), weight)
         o_grad[0, :, 512 * j : 512 * j + 512] = part[:52].astype(BF)
 
-    def u64(kx, ks):
-        return upd.at[rows(at(x, kx) * 512 + c * 256 + at(s, ks) * 64, 64)]
-
-    def u256(kx, kc):
-        return upd.at[rows(at(x, kx) * 512 + (1 - c if kc else c) * 256, 256)]
+    across = [(kx, kc) for kx in (2, 1, 3, 0) for kc in (1, 0) if kx or kc]
+
+    def u64(kx, ks, kc=0):
+        start = at(x, kx) * 512 + (1 - c if kc else c) * 256 + at(s, ks) * 64
+        return upd.at[rows(start, 64)]
 
     for ks in (0, 1, 3, 2):
         for kz in (1, 2, 3, 0):
             if ks or kz:
                 source = rows(base + place(4 - ks, 4 - kz), 16)
                 recv(f"u{ks}{kz}", upd.at[source])
-        for kx in (2, 1, 3):
-            send(f"ux{kx}{ks}", u64(0, 4 - ks), u64(0, 4 - ks), dev(kx=kx))
-    send("uc0", u256(0, 0), u256(0, 0), other)
+        for kx, kc in across:
+            send(f"ux{kx}{kc}{ks}", u64(0, 4 - ks), u64(0, 4 - ks), dev(kx=kx, kc=kc))
     own = upd[rows(base, 256), :].astype(F32)
     sq[...] = jnp.sum((own * own).reshape(32, 8, COLS), axis=0)
     for k in (1, 3, 2):
@@ -405,22 +407,16 @@
     for k in (1, 3, 2):
         recv(f"sy{k}", ysq.at[3 - k])
     xs[...] = sq[...] + ysq[0] + ysq[1] + ysq[2]
-    across = [(kx, kc) for kx in (2, 1, 3, 0) for kc in (1, 0) if kx or kc]
     for i, (kx, kc) in enumerate(across):
         send(f"sx{kx}{kc}", xs, xsq.at[i], dev(kx=kx, kc=kc))
-    for kx in (1, 3, 2):
-        for ks in (0, 1, 3, 2):
-            recv(f"ux{kx}{ks}", u64(4 - kx, 4 - ks))
-        send(f"uc{kx}", u256(4 - kx, 0), u256(4 - kx, 0), other)
     everything = xs[...]
     for i, (kx, kc) in enumerate(across):
         recv(f"sx{kx}{kc}", xsq.at[i])
         everything = everything + xsq[i]
     o_sq[...] = everything
-    drain(len(sent) - 3)
-    recv("uc0", u256(0, 1))
-    for kx in (1, 3, 2):
-        recv(f"uc{kx}", u256(4 - kx, 1))
+    for ks in (0, 1, 3, 2):
+        for kx, kc in across:
+            recv(f"ux{kx}{kc}{ks}", u64(4 - kx, 4 - ks, kc))
     o_upd[...] = upd[...]
     drain(len(sent))
 
@@ -447,7 +443,7 @@
         vm((112, COLS), BF), vm((96, COLS), BF), vm((112, COLS), BF), vm((96, COLS), BF),
         vm((112, COLS), BF), vm((96, COLS), BF),
         vm((ROWS, COLS), F32), vm((8 * ROWS, COLS), BF), vm((8 * ROWS, 256), BF),
-        vm((256, 8 * ROWS), BF), vm((256, COLS), F32), vm((256, COLS), BF),
+        vm((256, 4 * ROWS), BF), vm((256, 4 * ROWS), BF), vm((256, COLS), F32), vm((256, COLS), BF),
         vm((15, 16, COLS), BF), vm((D, COLS), BF),
         vm((8, 128), F32), vm((3, 8, 128), F32), vm((8, 128), F32), vm((7, 8, 128), F32),
         vm((4, 64, COLS), BF), vm((4, 64, COLS), BF),

time: 82.8 us -> 83.7 us (1.011)
    pallas_call x1, Pallas kernels: 80.3 us -> 81.1 us  [per_device(): pl.pallas_call(kernel, out_shape=(jax.ShapeDtypeStruct((1, 52, D), BF), j...]
where the time goes in v10:
time: 83.7 us; the launch traced here: 83.5 us
  Pallas kernels  82.2 us (98%)
  between operations  1.29 us (2%)
    pallas_call x1, Pallas kernels, per_device(): pl.pallas_call(kernel, out_shape=(jax.ShapeDtypeStruct((1, 52, D), BF), j...  81.1 us

profile of v10, /device:TPU:1, one launch (start us, length us, event | category | flops | bytes accessed | tf_op | source)
XLA Modules:
  0.0 83.5 jit_solution(6187374629560108631)
XLA Ops:
  1.3 81.1 %shard_map.95 = (bf16[1,52,2048]{2,1,0:T(8,128)(2,1)S(1)}, bf16[2048,128]{1,0:T(8,128)(2,1)S(1)}, f32[8,128]{1,0:T(8,128)S(1)}) custom-call(s32[1]{0:T(128)S(6)} %copy.10.len_ref, s32[1,3]{1,0:T(1,128)} %view_h.1, bf16[1,208,2048]{2,1,0:T(8,128)(2,1)} %hid_h.1, bf16[2048,128]{1,0:T(8,128)(2,1)} %w_h.1, bf16[1,300,1024]{2,1,0:T(8,128)(2,1)} %act_h.1, ...), custom_call_target="tpu_custom_call" | custom-call | tf_op jit(solution)/shard_map/pallas_call | solution.py:456
  82.4 1.1 %shard_map.96 = (bf16[1,52,2048]{2,1,0:T(8,128)(2,1)}, bf16[2048,128]{1,0:T(8,128)(2,1)}) custom-call(bf16[1,52,2048]{2,1,0:T(8,128)(2,1)S(1)} %get-tuple-element.5.grad_ref, bf16[2048,128]{1,0:T(8,128)(2,1)S(1)} %get-tuple-element.6.raw_ref, f32[8,128]{1,0:T(8,128)S(1)} %get-tuple-element.7.sq_ref), custom_call_target="tpu_custom_call" | custom-call | tf_op jit(solution)/shard_map/pallas_call | solution.py:471

commit v11 on v9

--- a/solution.py
+++ b/solution.py
@@ -41,7 +41,7 @@
     hid_v, wg, act_v, wq_v, wakv_v, cot_v, kv, akv, qs, gs, qt, gt, e_s, d_s,
     dkv, st, yb,
     rr, zst, za0, za1, zb0, zb1, zc0, zc1,
-    dres, gbuf, hx, hxt, tf, ts, zr, upd,
+    dres, gbuf, hx, hxa, hxb, tf, ts, zr, upd,
     sq, ysq, xs, xsq, ds, dr,
     view_ref, lsem, ssem, rsem,
 ):
@@ -125,8 +125,8 @@
         for k in (2, 1, 3):
             send(f"y{r}{k}{h}", block, block, dev(km=k))
 
-    def ywait(r):
-        for h in (0, 1):
+    def ywait(r, halves=(0, 1)):
+        for h in halves:
             r0, n = HALF[h]
             for k in (1, 3, 2):
                 recv(f"y{r}{k}{h}", kv.at[r, at(m, 4 - k), pl.ds(r0, n)])
@@ -150,7 +150,7 @@
     ysend(0, 1)
 
     def slot(rx, rc):
-        return pl.ds((rx * 2 + rc) * ROWS, ROWS)
+        return pl.ds((rc * 4 + rx) * ROWS, ROWS)
 
     def hidden_columns(kx, kc):
         j = at(x, kx) * 2 + (1 - c if kc else c)
@@ -161,6 +161,7 @@
             send(f"hx{kx}{kc}", hid_v.at[:, hidden_columns(kx, kc)],
                  hx.at[slot(4 - kx, kc)], dev(kx=kx, kc=kc))
 
+    first = len(sent)
     send_hidden(1)
     send_hidden(3)
     send("hx01", hid_v.at[:, hidden_columns(0, 1)], hx.at[slot(0, 1)], other)
@@ -184,6 +185,10 @@
     qt[...] = qs[...].T
     gt[...] = gs[...].T
 
+    def half(h):
+        r0, n = HALF[h]
+        return pl.ds(r0, n)
+
     block_max, block_sum, block_dot = {}, {}, {}
 
     def attend(r, keys, values, mask, e_ref, d_ref):
@@ -222,16 +227,19 @@
 
     loads[7].wait()
 
-    def attend_prefix(r):
-        p = at(s, r) * ROWS + lax.broadcasted_iota(jnp.int32, (ROWS, 1), 0)
+    def attend_prefix(r, part=None):
+        r0, n = (0, ROWS) if part is None else HALF[part]
+        p = at(s, r) * ROWS + r0 + lax.broadcasted_iota(jnp.int32, (n, 1), 0)
         usable = jnp.where(p >= VIEWS * VIEW_TOK, jnp.where(p - VIEWS * VIEW_TOK < len_ref[0], 1, 0), 0)
         for v in range(VIEWS):
             inside = jnp.where(p >= v * VIEW_TOK, 1, 0) * jnp.where(p < (v + 1) * VIEW_TOK, 1, 0)
             usable = usable + inside * jnp.where(view_ref[0, v] == 1, 1, 0)
         ceiling = jnp.where(usable > 0, -NEG, NEG)
+        some = pl.ds(r0, n)
         attend(
-            r, wide(kv[r, 0], kv[r, 1]), wide(kv[r, 2], kv[r, 3]),
-            lambda scores: jnp.minimum(scores, ceiling), e_s.at[r], d_s.at[r],
+            r if part is None else (r, part),
+            wide(kv[r, 0, some, :], kv[r, 1, some, :]), wide(kv[r, 2, some, :], kv[r, 3, some, :]),
+            lambda scores: jnp.minimum(scores, ceiling), e_s.at[r, some], d_s.at[r, some],
         )
 
     for i in (2, 3):
@@ -253,24 +261,27 @@
     attend_prefix(3)
     ywait(1)
     attend_prefix(1)
-    ywait(2)
-    attend_prefix(2)
-
-    blocks = ("a", 0, 1, 2, 3)
-    top = block_max["a"]
-    for r in (0, 1, 2, 3):
-        top = jnp.maximum(top, block_max[r])
-    factor = {r: jnp.exp(block_max[r] - top) for r in blocks}
-    total = sum(factor[r] * block_sum[r] for r in blocks)
+    drain(first)
+
+    def merge(parts):
+        top = block_max[parts[0]]
+        for i in parts[1:]:
+            top = jnp.maximum(top, block_max[i])
+        scaled = [jnp.exp(block_max[i] - top) for i in parts]
+        total = sum(f * block_sum[i] for f, i in zip(scaled, parts))
+        return top, total, sum(f * block_dot[i] for f, i in zip(scaled, parts))
+
+    block_max["m"], block_sum["m"], block_dot["m"] = merge(("a", 0, 1, 3))
+    for h in (0, 1):
+        ywait(2, (h,))
+        attend_prefix(2, h)
+    top, total, row_dot = merge(("m", (2, 0), (2, 1)))
     inverse = 1.0 / total
-    row_dot = sum(factor[r] * block_dot[r] for r in blocks) * inverse
-
-    def half(h):
-        r0, n = HALF[h]
-        return pl.ds(r0, n)
+    row_dot = row_dot * inverse
 
     def gradients(r, h):
-        p = e_s[r, half(h), :] * (factor[r] * inverse)
+        largest = block_max[(2, h) if r == 2 else r]
+        p = e_s[r, half(h), :] * (jnp.exp(largest - top) * inverse)
         d = p * (d_s[r, half(h), :] - row_dot)
         dk = dot(d.astype(BF), qs[...])
         dv = dot(p.astype(BF), gs[...])
@@ -297,7 +308,6 @@
         send(f"z{i}", zst.at[r, half(h)], target, zm if i % 2 else zp)
         if i < 2:
             gradients(0, i)
-    early = len(sent)
     for i, (r, h), arrived, target in ((4, order[4], za0, zc0), (5, order[5], za1, zc1)):
         piece = finish(r, h)
         recv(f"z{i - 4}", arrived)
@@ -316,8 +326,8 @@
         for kc in (0, 1):
             recv(f"hx{kx}{kc}", hx.at[slot(4 - kx, kc)])
     recv("hx01", hx.at[slot(0, 1)])
-    hxt[...] = hx[...].T
-    drain(early)
+    hxa[...] = hx[0 : 4 * ROWS, :].T
+    hxb[...] = hx[4 * ROWS : 8 * ROWS, :].T
 
     def block(rx, rc):
         return gbuf.at[slot(rx, rc)]
@@ -345,11 +355,13 @@
     for kx in (1, 3, 2):
         recv(f"g{kx}", block(4 - kx, 0))
         send(f"gc{kx}", block(4 - kx, 0), block(4 - kx, 1), other)
+    tf[...] = dot(hxa[...], gbuf[0 : 4 * ROWS, :])
     for kx in (0, 1, 3, 2):
         recv(f"gc{kx}", block((4 - kx) % 4, 1))
 
-    tf[...] = dot(hxt[...], gbuf[...])
-    ts[...] = tf[...].astype(BF)
+    part = tf[...] + dot(hxb[...], gbuf[4 * ROWS : 8 * ROWS, :])
+    tf[...] = part
+    ts[...] = part.astype(BF)
 
     def rows(start, n):
         return pl.ds(pl.multiple_of(start, n), n)
@@ -447,7 +459,7 @@
         vm((112, COLS), BF), vm((96, COLS), BF), vm((112, COLS), BF), vm((96, COLS), BF),
         vm((112, COLS), BF), vm((96, COLS), BF),
         vm((ROWS, COLS), F32), vm((8 * ROWS, COLS), BF), vm((8 * ROWS, 256), BF),
-        vm((256, 8 * ROWS), BF), vm((256, COLS), F32), vm((256, COLS), BF),
+        vm((256, 4 * ROWS), BF), vm((256, 4 * ROWS), BF), vm((256, COLS), F32), vm((256, COLS), BF),
         vm((15, 16, COLS), BF), vm((D, COLS), BF),
         vm((8, 128), F32), vm((3, 8, 128), F32), vm((8, 128), F32), vm((7, 8, 128), F32),
         vm((4, 64, COLS), BF), vm((4, 64, COLS), BF),

time: 82.8 us -> 82.5 us (level)
  no operation moved by 1% of the time
where the time goes in v11:
time: 82.5 us; the launch traced here: 82.4 us
  Pallas kernels  81.1 us (98%)
  between operations  1.29 us (2%)
    pallas_call x1, Pallas kernels, per_device(): pl.pallas_call(kernel, out_shape=(jax.ShapeDtypeStruct((1, 52, D), BF), j...  80 us

profile of v11, /device:TPU:1, one launch (start us, length us, event | category | flops | bytes accessed | tf_op | source)
XLA Modules:
  0.0 82.4 jit_solution(13877901624369331258)
XLA Ops:
  1.3 80.0 %shard_map.95 = (bf16[1,52,2048]{2,1,0:T(8,128)(2,1)S(1)}, bf16[2048,128]{1,0:T(8,128)(2,1)S(1)}, f32[8,128]{1,0:T(8,128)S(1)}) custom-call(s32[1]{0:T(128)S(6)} %copy.10.len_ref, s32[1,3]{1,0:T(1,128)} %view_h.1, bf16[1,208,2048]{2,1,0:T(8,128)(2,1)} %hid_h.1, bf16[2048,128]{1,0:T(8,128)(2,1)} %w_h.1, bf16[1,300,1024]{2,1,0:T(8,128)(2,1)} %act_h.1, ...), custom_call_target="tpu_custom_call" | custom-call | tf_op jit(solution)/shard_map/pallas_call | solution.py:472
  81.3 1.1 %shard_map.96 = (bf16[1,52,2048]{2,1,0:T(8,128)(2,1)}, bf16[2048,128]{1,0:T(8,128)(2,1)}) custom-call(bf16[1,52,2048]{2,1,0:T(8,128)(2,1)S(1)} %get-tuple-element.5.grad_ref, bf16[2048,128]{1,0:T(8,128)(2,1)S(1)} %get-tuple-element.6.raw_ref, f32[8,128]{1,0:T(8,128)S(1)} %get-tuple-element.7.sq_ref), custom_call_target="tpu_custom_call" | custom-call | tf_op jit(solution)/shard_map/pallas_call | solution.py:487

commit v12 on v11

--- a/solution.py
+++ b/solution.py
@@ -20,7 +20,7 @@
 NEG = -3.0e38
 HALF = ((0, 112), (112, 96))
 PART = ((0, 64), (64, 48), (112, 48), (160, 48))
-N_SEMS = 160
+N_SEMS = 200
 
 
 def dot(a, b):
@@ -125,11 +125,21 @@
         for k in (2, 1, 3):
             send(f"y{r}{k}{h}", block, block, dev(km=k))
 
-    def ywait(r, halves=(0, 1)):
-        for h in halves:
+    def ywait(r):
+        for h in (0, 1):
             r0, n = HALF[h]
             for k in (1, 3, 2):
                 recv(f"y{r}{k}{h}", kv.at[r, at(m, 4 - k), pl.ds(r0, n)])
+
+    def ylast(i):
+        for k in (2, 1, 3):
+            send(f"yl{k}{i}", kvp(2, i), kvp(2, i), dev(km=k))
+
+    def ylast_wait(h):
+        for i in (2 * h, 2 * h + 1):
+            r0, n = PART[i]
+            for k in (1, 3, 2):
+                recv(f"yl{k}{i}", kv.at[2, at(m, 4 - k), pl.ds(r0, n)])
 
     loads[1].wait()
     loads[0].wait()
@@ -250,12 +260,9 @@
     ysend(1, 0)
     ywait(0)
     attend_prefix(0)
-    for i in (0, 1):
+    for i in (0, 2, 1, 3):
         recv(f"zf{i}", kvp(2, i))
-    ysend(2, 0)
-    for i in (2, 3):
-        recv(f"zf{i}", kvp(2, i))
-    ysend(2, 1)
+        ylast(i)
     send_hidden(2)
     ywait(3)
     attend_prefix(3)
@@ -273,7 +280,7 @@
 
     block_max["m"], block_sum["m"], block_dot["m"] = merge(("a", 0, 1, 3))
     for h in (0, 1):
-        ywait(2, (h,))
+        ylast_wait(h)
         attend_prefix(2, h)
     top, total, row_dot = merge(("m", (2, 0), (2, 1)))
     inverse = 1.0 / total

time: 82.5 us -> 82.5 us (level)
  no operation moved by 1% of the time
where the time goes in v12:
time: 82.5 us; the launch traced here: 82.3 us
  Pallas kernels  81 us (98%)
  between operations  1.29 us (2%)
    pallas_call x1, Pallas kernels, per_device(): pl.pallas_call(kernel, out_shape=(jax.ShapeDtypeStruct((1, 52, D), BF), j...  79.9 us

profile of v12, /device:TPU:1, one launch (start us, length us, event | category | flops | bytes accessed | tf_op | source)
XLA Modules:
  0.0 82.3 jit_solution(8773065911283702581)
XLA Ops:
  1.3 79.9 %shard_map.95 = (bf16[1,52,2048]{2,1,0:T(8,128)(2,1)S(1)}, bf16[2048,128]{1,0:T(8,128)(2,1)S(1)}, f32[8,128]{1,0:T(8,128)S(1)}) custom-call(s32[1]{0:T(128)S(6)} %copy.10.len_ref, s32[1,3]{1,0:T(1,128)} %view_h.1, bf16[1,208,2048]{2,1,0:T(8,128)(2,1)} %hid_h.1, bf16[2048,128]{1,0:T(8,128)(2,1)} %w_h.1, bf16[1,300,1024]{2,1,0:T(8,128)(2,1)} %act_h.1, ...), custom_call_target="tpu_custom_call" | custom-call | tf_op jit(solution)/shard_map/pallas_call | solution.py:479
  81.2 1.1 %shard_map.96 = (bf16[1,52,2048]{2,1,0:T(8,128)(2,1)}, bf16[2048,128]{1,0:T(8,128)(2,1)}) custom-call(bf16[1,52,2048]{2,1,0:T(8,128)(2,1)S(1)} %get-tuple-element.5.grad_ref, bf16[2048,128]{1,0:T(8,128)(2,1)S(1)} %get-tuple-element.6.raw_ref, f32[8,128]{1,0:T(8,128)S(1)} %get-tuple-element.7.sq_ref), custom_call_target="tpu_custom_call" | custom-call | tf_op jit(solution)/shard_map/pallas_call | solution.py:494

commit v13 on v12

--- a/solution.py
+++ b/solution.py
@@ -378,9 +378,6 @@
 
     for i, (ks, kz) in enumerate(along_z):
         send(f"t{ks}{kz}", ts.at[rows(place(ks, kz), 16)], zr.at[i], dev(ks=ks, kz=kz))
-    for k in (1, 3, 2):
-        recv(f"w{k}", wpart(c, 4 - k))
-        send(f"wc{k}", wpart(c, 4 - k), wpart(c, 4 - k), other)
     late = len(sent)
     base = (x * 2 + c) * 256
     piece = tf[rows(z * 16, 16), :]
@@ -391,16 +388,10 @@
     mine[...] = piece.astype(BF)
     for ks, kz in along_z:
         send(f"u{ks}{kz}", mine, mine, dev(ks=ks, kz=kz))
+    for k in (1, 3, 2):
+        recv(f"w{k}", wpart(c, 4 - k))
+        send(f"wc{k}", wpart(c, 4 - k), wpart(c, 4 - k), other)
     drain(late)
-
-    for k in (1, 3, 2):
-        recv(f"wc{k}", wpart(1 - c, 4 - k))
-    for k in (1, 3, 2):
-        recv(f"dy{k}", dr.at[at(m, 4 - k)])
-    for j in range(4):
-        weight = wide(*[wg[k, 512 * j : 512 * j + 512, :] for k in range(4)])
-        part = dot_nt(wide(dr[0], dr[1], dr[2], dr[3]), weight)
-        o_grad[0, :, 512 * j : 512 * j + 512] = part[:52].astype(BF)
 
     def u64(kx, ks):
         return upd.at[rows(at(x, kx) * 512 + c * 256 + at(s, ks) * 64, 64)]
@@ -420,6 +411,15 @@
     sq[...] = jnp.sum((own * own).reshape(32, 8, COLS), axis=0)
     for k in (1, 3, 2):
         send(f"sy{k}", sq, ysq.at[3 - k], dev(km=k))
+
+    for k in (1, 3, 2):
+        recv(f"wc{k}", wpart(1 - c, 4 - k))
+    for k in (1, 3, 2):
+        recv(f"dy{k}", dr.at[at(m, 4 - k)])
+    for j in range(4):
+        weight = wide(*[wg[k, 512 * j : 512 * j + 512, :] for k in range(4)])
+        part = dot_nt(wide(dr[0], dr[1], dr[2], dr[3]), weight)
+        o_grad[0, :, 512 * j : 512 * j + 512] = part[:52].astype(BF)
 
     for k in (1, 3, 2):
         recv(f"sy{k}", ysq.at[3 - k])

time: 82.5 us -> 82.5 us (level)
  no operation moved by 1% of the time
where the time goes in v13:
time: 82.5 us; the launch traced here: 82.3 us
  Pallas kernels  81 us (98%)
  between operations  1.29 us (2%)
    pallas_call x1, Pallas kernels, per_device(): pl.pallas_call(kernel, out_shape=(jax.ShapeDtypeStruct((1, 52, D), BF), j...  79.9 us

profile of v13, /device:TPU:1, one launch (start us, length us, event | category | flops | bytes accessed | tf_op | source)
XLA Modules:
  0.0 82.3 jit_solution(12975801556312559475)
XLA Ops:
  1.3 79.9 %shard_map.95 = (bf16[1,52,2048]{2,1,0:T(8,128)(2,1)S(1)}, bf16[2048,128]{1,0:T(8,128)(2,1)S(1)}, f32[8,128]{1,0:T(8,128)S(1)}) custom-call(s32[1]{0:T(128)S(6)} %copy.10.len_ref, s32[1,3]{1,0:T(1,128)} %view_h.1, bf16[1,208,2048]{2,1,0:T(8,128)(2,1)} %hid_h.1, bf16[2048,128]{1,0:T(8,128)(2,1)} %w_h.1, bf16[1,300,1024]{2,1,0:T(8,128)(2,1)} %act_h.1, ...), custom_call_target="tpu_custom_call" | custom-call | tf_op jit(solution)/shard_map/pallas_call | solution.py:479
  81.2 1.1 %shard_map.96 = (bf16[1,52,2048]{2,1,0:T(8,128)(2,1)}, bf16[2048,128]{1,0:T(8,128)(2,1)}) custom-call(bf16[1,52,2048]{2,1,0:T(8,128)(2,1)S(1)} %get-tuple-element.5.grad_ref, bf16[2048,128]{1,0:T(8,128)(2,1)S(1)} %get-tuple-element.6.raw_ref, f32[8,128]{1,0:T(8,128)S(1)} %get-tuple-element.7.sq_ref), custom_call_target="tpu_custom_call" | custom-call | tf_op jit(solution)/shard_map/pallas_call | solution.py:494
